TPU v7x, 128 devices: a whole 4x4x4 slice. The times are simulated.
128 devices in a mesh: dp: 8 (over z_lo, y), mp: 16 (over z_hi, x, core).
Axes of the slice: x: 4, y: 4, z: 4 (z_hi: 2, z_lo: 2; z = z_hi * 2 + z_lo), core: 2. Of those that a mesh axis runs over, the one named last changes fastest.
Arguments:
- tokens: bfloat16 [5120, 4096], P(('dp', 'mp')), may hold values from -24 to 24
- w_gate: bfloat16 [4096, 8192], P(None, 'mp'), may hold values from -0.09375 to 0.09375
- w_up: bfloat16 [4096, 8192], P(None, 'mp'), may hold values from -0.09375 to 0.09375
- w_down: bfloat16 [8192, 4096], P('mp'), may hold values from -0.0625 to 0.0625
- cotangent: bfloat16 [5120, 4096], P(('dp', 'mp')), may hold values from -6 to 6
Outputs:
- mixed: bfloat16 [5120, 4096], P(('dp', 'mp'))
- input_grad: bfloat16 [5120, 4096], P(('dp', 'mp'))
- grad_gate: bfloat16 [4096, 8192], P('dp', 'mp')
- grad_up: bfloat16 [4096, 8192], P('dp', 'mp')
- grad_down: bfloat16 [8192, 4096], P('mp', 'dp')
All inputs are finite; a program needn't handle non-finite values.
Results may differ from a plain program's by a relative error of at most 0.019.
Values may be sent and summed in bfloat16 or wider, within the bound.
A program may use at most 192 MiB of HBM per device.

v0:
```python
import jax
import jax.numpy as jnp
from jax import lax
from jax.sharding import PartitionSpec as P


def contract_rows(left, right):
    return lax.dot_general(
        left, right, (((0,), (0,)), ((), ())), preferred_element_type=jnp.float32
    )


def contract_cols(left, right):
    return lax.dot_general(
        left, right, (((1,), (1,)), ((), ())), preferred_element_type=jnp.float32
    )


def on_device(tokens, w_gate, w_up, w_down, cotangent):
    panel = w_gate.shape[1]
    gathered = lax.all_gather(tokens, "mp", axis=0, tiled=True)
    gate = jnp.dot(gathered, w_gate, preferred_element_type=jnp.float32)
    up = jnp.dot(gathered, w_up, preferred_element_type=jnp.float32)
    swish = jax.nn.silu(gate)
    hidden = (swish * up).astype(jnp.bfloat16)
    mixed = lax.psum_scatter(
        jnp.dot(hidden, w_down, preferred_element_type=jnp.float32).astype(jnp.bfloat16),
        "mp",
        scatter_dimension=0,
        tiled=True,
    )
    upstream = lax.all_gather(cotangent, "mp", axis=0, tiled=True)
    dhidden = contract_cols(upstream, w_down)
    sigma = jax.nn.sigmoid(gate)
    dgate = (dhidden * up * sigma * (1.0 + gate * (1.0 - sigma))).astype(jnp.bfloat16)
    dup = (dhidden * swish).astype(jnp.bfloat16)
    input_grad = lax.psum_scatter(
        (contract_cols(dgate, w_gate) + contract_cols(dup, w_up)).astype(jnp.bfloat16),
        "mp",
        scatter_dimension=0,
        tiled=True,
    )
    summed = lax.psum_scatter(
        jnp.concatenate(
            [
                contract_rows(gathered, dgate),
                contract_rows(gathered, dup),
                contract_rows(upstream, hidden),
            ],
            axis=1,
        ).astype(jnp.bfloat16),
        "dp",
        scatter_dimension=0,
        tiled=True,
    ).astype(jnp.float32)
    grad_gate = summed[:, :panel]
    grad_up = summed[:, panel : 2 * panel]
    grad_down = summed[:, 2 * panel :].T
    return (
        mixed,
        input_grad,
        grad_gate.astype(jnp.bfloat16),
        grad_up.astype(jnp.bfloat16),
        grad_down.astype(jnp.bfloat16),
    )


def solution(mesh):
    in_specs = (
        P(("dp", "mp"), None),
        P(None, "mp"),
        P(None, "mp"),
        P("mp", None),
        P(("dp", "mp"), None),
    )
    out_specs = (
        P(("dp", "mp"), None),
        P(("dp", "mp"), None),
        P("dp", "mp"),
        P("dp", "mp"),
        P("mp", "dp"),
    )
    return jax.shard_map(
        on_device, mesh=mesh, in_specs=in_specs, out_specs=out_specs, check_vma=False
    )
```

profile of v0, /device:TPU:1, one launch (start us, length us, event | category | flops | bytes accessed | tf_op | source)
XLA Modules:
  0.0 487.2 jit_solution(3796393850004343165)
XLA Ops:
  7.2 0.7 all-gather.3.cloned.1.call-update
  7.9 0.0 all-gather.5.cloned.1.call-start
  7.9 0.7 all-gather.5.cloned.1.call-update
  8.6 0.0 reduce-scatter.8.cloned.1.call-start
  8.7 65.3 %all-gather.3.cloned.1.call-done = bf16[640,4096]{1,0:T(8,128)(2,1)} async-done(((bf16[40,4096]{1,0:T(8,128)(2,1)}), bf16[640,4096]{1,0:T(8,128)(2,1)}) %all-gather.3.cloned.1.call-update) | async-done | bytes 5242896 | tf_op jit(solution)/shard_map/all_gather | solution.py:21
  74.0 7.9 %fusion.5 = f32[640,512]{1,0:T(8,128)} fusion(bf16[640,4096]{1,0:T(8,128)(2,1)} %all-gather.3.cloned.1.call-done, bf16[4096,512]{1,0:T(8,128)(2,1)} %param.7), kind=kOutput, calls=%fused_computation.16 | convolution fusion | flops 2684354560 | bytes 10747904 | tf_op jit(solution)/shard_map/dot_general | solution.py:23
  81.9 3.9 fusion.4
  85.9 49.2 %all-gather.5.cloned.1.call-done = bf16[640,4096]{1,0:T(8,128)(2,1)} async-done(((bf16[40,4096]{1,0:T(8,128)(2,1)}), bf16[640,4096]{1,0:T(8,128)(2,1)}) %all-gather.5.cloned.1.call-update) | async-done | bytes 5242896 | tf_op jit(solution)/shard_map/all_gather | solution.py:32
  135.1 8.0 %multiply_convert_fusion = (bf16[640,512]{1,0:T(8,128)(2,1)S(1)}, bf16[640,512]{1,0:T(8,128)(2,1)S(1)}, bf16[640,512]{1,0:T(8,128)(2,1)S(1)}) fusion(f32[640,512]{1,0:T(8,128)} %fusion.4, f32[640,512]{1,0:T(8,128)} %fusion.5, bf16[640,4096]{1,0:T(8,128)(2,1)} %all-gather.5.cloned.1.call-done, bf16[512,4096]{1,0:T(8,128)(2,1)} %param.8), kind=kOutput, calls=%fused_computation.9 | convolution fusion | flops 2689269760 | bytes 14024704 | tf_op jit(solution)/shard_map/dot_general | solution.py:14
  143.1 3.9 fusion.2
  147.0 6.3 %fusion.1 = bf16[4096,512]{0,1:T(8,128)(2,1)S(1)} fusion(bf16[640,512]{1,0:T(8,128)(2,1)S(1)} %get-tuple-element.10, bf16[640,4096]{1,0:T(8,128)(2,1)} %all-gather.3.cloned.1.call-done), kind=kOutput, calls=%fused_computation.7 | convolution fusion | flops 2686451712 | bytes 10092544 | tf_op jit(solution)/shard_map/dot_general | solution.py:8
  153.3 3.7 fusion
  157.1 17.8 %pad_maximum_fusion = bf16[4096,1536]{0,1:T(8,128)(2,1)} fusion(bf16[4096,512]{0,1:T(8,128)(2,1)S(1)} %fusion.2, bf16[4096,512]{0,1:T(8,128)(2,1)S(1)} %fusion.1, bf16[4096,512]{0,1:T(8,128)(2,1)S(1)} %fusion), kind=kLoop, calls=%fused_computation | loop fusion | flops 37748736 | bytes 25165824 | tf_op jit(solution)/shard_map/concatenate | solution.py:44
  174.8 0.0 reduce-scatter.4.cloned.1.call-start
  174.9 6.9 %convolution_convert_fusion = bf16[640,4096]{1,0:T(8,128)(2,1)} fusion(bf16[640,512]{1,0:T(8,128)(2,1)S(1)} %get-tuple-element.12, bf16[512,4096]{1,0:T(8,128)(2,1)} %param.8), kind=kOutput, calls=%fused_computation.2 | convolution fusion | flops 2686976000 | bytes 10092544 | tf_op jit(solution)/shard_map/dot_general | solution.py:27
  181.8 0.0 reduce-scatter.6.cloned.1.call-start
  181.9 5.5 %fusion.6 = f32[640,4096]{1,0:T(8,128)S(1)} fusion(bf16[640,512]{1,0:T(8,128)(2,1)S(1)} %get-tuple-element.11, bf16[4096,512]{1,0:T(8,128)(2,1)} %param.6), kind=kOutput, calls=%fused_computation.17 | convolution fusion | flops 2684354560 | bytes 15335424 | tf_op jit(solution)/shard_map/dot_general | solution.py:14
  187.4 4.8 add_convert_fusion
  192.2 113.4 %reduce-scatter.8.cloned.1.call-done = bf16[512,1536]{0,1:T(8,128)(2,1)} async-done(((bf16[4096,1536]{0,1:T(8,128)(2,1)}), bf16[512,1536]{0,1:T(8,128)(2,1)}) %reduce-scatter.8.cloned.1.call-update) | async-done | bytes 1572880 | tf_op jit(solution)/shard_map/reduce_scatter | solution.py:43
  305.6 2.3 slice_bitcast_fusion
  307.9 1.0 copy.11
  308.9 1.0 copy.10
  309.9 82.6 %reduce-scatter.4.cloned.1.call-done = bf16[40,4096]{1,0:T(8,128)(2,1)} async-done(((bf16[640,4096]{1,0:T(8,128)(2,1)}), bf16[40,4096]{1,0:T(8,128)(2,1)}) %reduce-scatter.4.cloned.1.call-update) | async-done | bytes 327696 | tf_op jit(solution)/shard_map/reduce_scatter | solution.py:26
  392.5 88.2 %reduce-scatter.6.cloned.1.call-done = bf16[40,4096]{1,0:T(8,128)(2,1)} async-done(((bf16[640,4096]{1,0:T(8,128)(2,1)}), bf16[40,4096]{1,0:T(8,128)(2,1)}) %reduce-scatter.6.cloned.1.call-update) | async-done | bytes 327696 | tf_op jit(solution)/shard_map/reduce_scatter | solution.py:37
  (17 shorter events, 0.1 us)
Async XLA Ops:
  7.2 66.9 %all-gather.3.cloned.1.call-start = ((), (), s32[]{:S(2)}) async-start(), calls=%async_computation.3 | async-start | bytes 5570560 | tf_op jit(solution)/shard_map/all_gather | solution.py:21
  7.9 127.2 %all-gather.5.cloned.1.call-start = ((), (), s32[]{:S(2)}) async-start(), calls=%async_computation.5 | async-start | bytes 5570560 | tf_op jit(solution)/shard_map/all_gather | solution.py:32
  8.6 297.0 %reduce-scatter.8.cloned.1.call-start = ((), (), s32[]{:S(2)}) async-start(), calls=%async_computation.7 | async-start | bytes 14155776 | tf_op jit(solution)/shard_map/reduce_scatter | solution.py:43
  74.0 7.9 %copy-start = (bf16[640,4096]{1,0:T(8,128)(2,1)S(1)}, bf16[640,4096]{1,0:T(8,128)(2,1)}, u32[]{:S(2)}) copy-start(bf16[640,4096]{1,0:T(8,128)(2,1)} %all-gather.3.cloned.1.call-done) | copy-start | bytes 15728644
  74.0 7.9 %copy-start.2 = (bf16[4096,512]{1,0:T(8,128)(2,1)S(1)}, bf16[4096,512]{1,0:T(8,128)(2,1)}, u32[]{:S(2)}) copy-start(bf16[4096,512]{1,0:T(8,128)(2,1)} %param.6) | copy-start | bytes 12582916
  135.1 8.0 %copy-start.1 = (bf16[640,4096]{1,0:T(8,128)(2,1)S(1)}, bf16[640,4096]{1,0:T(8,128)(2,1)}, u32[]{:S(2)}) copy-start(bf16[640,4096]{1,0:T(8,128)(2,1)} %all-gather.5.cloned.1.call-done) | copy-start | bytes 15728644
  143.0 10.2 %slice-start = ((s8[5242880]{0:T(1024)(128)(4,1)}), s8[4194304]{0:T(1024)(128)(4,1)S(1)}, s32[]{:S(2)}) async-start(s8[5242880]{0:T(1024)(128)(4,1)} %bitcast.26), calls=%async_computation.8 | async-start | bytes 8388608
  147.0 6.3 %slice-start.1 = ((s8[5242880]{0:T(1024)(128)(4,1)}), s8[1048576]{0:T(1024)(128)(4,1)S(1)}, s32[]{:S(2)}) async-start(s8[5242880]{0:T(1024)(128)(4,1)} %bitcast.26), calls=%async_computation.9 | async-start | bytes 2097152
  174.8 217.6 %reduce-scatter.4.cloned.1.call-start = ((), (), s32[]{:S(2)}) async-start(), calls=%async_computation.4 | async-start | bytes 5570560 | tf_op jit(solution)/shard_map/reduce_scatter | solution.py:26
  181.8 298.9 %reduce-scatter.6.cloned.1.call-start = ((), (), s32[]{:S(2)}) async-start(), calls=%async_computation.6 | async-start | bytes 5570560 | tf_op jit(solution)/shard_map/reduce_scatter | solution.py:37
  181.9 5.5 %copy-start.3 = (bf16[4096,512]{1,0:T(8,128)(2,1)S(1)}, bf16[4096,512]{1,0:T(8,128)(2,1)}, u32[]{:S(2)}) copy-start(bf16[4096,512]{1,0:T(8,128)(2,1)} %param.7) | copy-start | bytes 12582916
Sparse Core Ops, SparseCore 0:
  10.4 63.5 all-gather.2
  76.5 58.5 all-gather.4
  175.0 130.5 reduce-scatter.7
  310.1 82.3 reduce-scatter.3
  397.0 83.6 reduce-scatter.5
where the time goes:
time: 488 us; the launch traced here: 487 us
  waiting for transfers between devices  400 us (82%)
  matrix products  50.9 us (10%)
  other arithmetic  17.8 us (4%)
  between operations  13.9 us (3%)
    reduce_scatter x1, waiting for transfers between devices, on_device(): lax.psum_scatter(jnp.concatenate([contract_rows(gathered, dgate), contrac...  113 us
    reduce_scatter x1, waiting for transfers between devices, on_device(): lax.psum_scatter((contract_cols(dgate, w_gate) + contract_cols(dup, w_up)...  88.2 us
    reduce_scatter x1, waiting for transfers between devices, on_device(): lax.psum_scatter(jnp.dot(hidden, w_down, preferred_element_type=jnp.float...  82.6 us
    all_gather x1, waiting for transfers between devices, on_device(): gathered = lax.all_gather(tokens, 'mp', axis=0, tiled=True)  65.3 us
    all_gather x1, waiting for transfers between devices, on_device(): upstream = lax.all_gather(cotangent, 'mp', axis=0, tiled=True)  49.2 us
    dot_general x3, matrix products, contract_cols(): lax.dot_general(left, right, (((1,), (1,)), ((), ())), preferred_element_...  18.2 us
    concatenate x1, other arithmetic, on_device(): jnp.concatenate([contract_rows(gathered, dgate), contract_rows(gathered,...  17.8 us
    dot_general x3, matrix products, contract_rows(): lax.dot_general(left, right, (((0,), (0,)), ((), ())), preferred_element_...  13.9 us
  transfers between devices with their start and end apart: 5, of which 5 were waited for; matrix products, arithmetic and copies ran while one was open for 7% of the time, Pallas kernels for 0%

commit v1 on v0

v1 whole, which is shorter than its diff:
```python
import jax
import jax.numpy as jnp
from jax import lax
from jax.experimental import pallas as pl
from jax.experimental.pallas import tpu as pltpu
from jax.sharding import PartitionSpec as P

MESH = pl.DeviceIdType.MESH
BF16 = jnp.bfloat16
F32 = jnp.float32
D = 4096
HALF = D // 2
LANE = HALF // 2
PANEL = 512
ROWS = 640
BLOCK = 80
PART = 320
MESSAGES = 110

OWN, LEFT, RIGHT, ACROSS, FAR, ACROSS_LEFT, ACROSS_RIGHT, ACROSS_FAR = range(8)


def mm(a, b):
    return jnp.dot(a, b, preferred_element_type=F32)


def mm_nt(a, b):
    return lax.dot_general(a, b, (((1,), (1,)), ((), ())), preferred_element_type=F32)


def add_into(dst, src, rows, step):
    @pl.loop(0, rows // step)
    def _(i):
        r = pl.ds(pl.multiple_of(i * step, step), step)
        dst[r, :] = (dst[r, :].astype(F32) + src[r, :].astype(F32)).astype(BF16)


def sum_to(dst, terms, rows, step):
    @pl.loop(0, rows // step)
    def _(i):
        r = pl.ds(pl.multiple_of(i * step, step), step)
        total = terms[0][r, :].astype(F32)
        for term in terms[1:]:
            total += term[r, :].astype(F32)
        dst[r, :] = total.astype(BF16)


def kernel(
    tok_hbm, wg_hbm, wu_hbm, wd_hbm, cot_hbm,
    mixed_out, ig_out, gate_out, up_out, down_out,
    wg, wu, wd, xc, hid, dg, du, lt, gf, uf, df, am, sm, pgu, pdo,
    mring, mz, gring, gz, dz, dring, t_in, fo,
    send_sem, recv_sem, local_sem, credit,
):
    dp, mp = lax.axis_index("dp"), lax.axis_index("mp")
    zl, y = dp // 4, dp % 4
    zh, x, c = mp // 8, (mp // 2) % 4, mp % 2
    x_right = (dp, zh * 8 + ((x + 1) % 4) * 2 + c)
    x_left = (dp, zh * 8 + ((x + 3) % 4) * 2 + c)
    z_across = (dp, (1 - zh) * 8 + x * 2 + c)
    sibling = (dp, zh * 8 + x * 2 + (1 - c))
    y_right = (zl * 4 + (y + 1) % 4, mp)
    y_left = (zl * 4 + (y + 3) % 4, mp)
    z_next = ((1 - zl) * 4 + y, mp)
    mine = pl.ds(pl.multiple_of(c * HALF, HALF), HALF)
    other = pl.ds(pl.multiple_of((1 - c) * HALF, HALF), HALF)

    pending = []

    def message(src, dst, device):
        n = len(pending)
        copy = pltpu.make_async_remote_copy(
            src_ref=src, dst_ref=dst, send_sem=send_sem.at[n], recv_sem=recv_sem.at[n],
            device_id=device, device_id_type=MESH,
        )
        pending.append(copy)
        return copy

    sent = set()

    def wait_send(copy):
        if id(copy) not in sent:
            sent.add(id(copy))
            copy.wait_send()

    weights = [
        pltpu.make_async_copy(src, dst, local_sem.at[n])
        for n, (src, dst) in enumerate(((wg_hbm, wg), (wu_hbm, wu), (wd_hbm, wd)))
    ]
    inputs = (tok_hbm, cot_hbm)
    own_rows = [pltpu.make_async_copy(inputs[a].at[:, mine], t_in.at[c, a], local_sem.at[3 + a]) for a in (0, 1)]
    for copy in own_rows:
        copy.start()
    for copy in weights:
        copy.start()

    barrier = pltpu.get_barrier_semaphore()
    partners = (x_right, x_left, z_across, sibling, y_right, y_left, z_next)
    for device in partners:
        pl.semaphore_signal(barrier, inc=1, device_id=device, device_id_type=MESH)
    pl.semaphore_wait(barrier, len(partners))

    rows_over = [message(inputs[a].at[:, other], t_in.at[c, a], sibling) for a in (0, 1)]
    for copy in rows_over:
        copy.start()

    def block(a, slot, cols=mine):
        return xc.at[a, pl.ds(slot * BLOCK, BLOCK), cols]

    def hand_over(a, slot):
        copy = message(block(a, slot), block(a, slot), sibling)
        copy.start()
        return copy

    to_right, to_left, to_across, relay, over = {}, {}, {}, {}, {}
    for a in (0, 1):
        own_rows[a].wait()
        rows_over[a].wait_recv()

        @pl.loop(0, HALF // PANEL)
        def _(j, a=a):
            cols = pl.ds(pl.multiple_of(j * PANEL, PANEL), PANEL)
            both = jnp.concatenate([t_in[0, a, :, cols].astype(F32), t_in[1, a, :, cols].astype(F32)], axis=0)
            xc[a, 0:BLOCK, pl.ds(pl.multiple_of(c * HALF + j * PANEL, PANEL), PANEL)] = both.astype(BF16)

        to_right[a, OWN] = message(block(a, OWN), block(a, LEFT), x_right)
        to_left[a, OWN] = message(block(a, OWN), block(a, RIGHT), x_left)
        to_across[a, OWN] = message(block(a, OWN), block(a, ACROSS), z_across)
        for copy in (to_right[a, OWN], to_left[a, OWN], to_across[a, OWN]):
            copy.start()
        over[a, OWN] = hand_over(a, OWN)

    def relay_far(a):
        if a == 0:
            relay[a] = message(block(a, LEFT), block(a, FAR), x_right)
        else:
            relay[a] = message(block(a, RIGHT), block(a, FAR), x_left)
        relay[a].start()

    for a in (0, 1):
        first, second = (to_right, to_left) if a == 0 else (to_left, to_right)
        first[a, OWN].wait_recv()
        relay_far(a)
        over[a, LEFT if a == 0 else RIGHT] = hand_over(a, LEFT if a == 0 else RIGHT)
        to_across[a, OWN].wait_recv()
        to_right[a, ACROSS] = message(block(a, ACROSS), block(a, ACROSS_LEFT), x_right)
        to_left[a, ACROSS] = message(block(a, ACROSS), block(a, ACROSS_RIGHT), x_left)
        to_right[a, ACROSS].start()
        to_left[a, ACROSS].start()
        over[a, ACROSS] = hand_over(a, ACROSS)
        second[a, OWN].wait_recv()
        over[a, RIGHT if a == 0 else LEFT] = hand_over(a, RIGHT if a == 0 else LEFT)

    def gate_up(r0):
        gf[...] = jnp.zeros_like(gf)
        uf[...] = jnp.zeros_like(uf)

        @pl.loop(0, 4)
        def _(k):
            ks = pl.ds(pl.multiple_of(k * 1024, 1024), 1024)
            rows = xc[0, r0:r0 + PART, ks]
            gf[...] += mm(rows, wg[ks, :])
            uf[...] += mm(rows, wu[ks, :])

    def backward(r0):
        df[...] = jnp.zeros_like(df)

        @pl.loop(0, 4)
        def _(k):
            ks = pl.ds(pl.multiple_of(k * 1024, 1024), 1024)
            df[...] += mm_nt(xc[1, r0:r0 + PART, ks], wd[:, ks])

        @pl.loop(0, PART // 32)
        def _(i):
            r = pl.ds(pl.multiple_of(i * 32, 32), 32)
            w = pl.ds(pl.multiple_of(r0 + i * 32, 32), 32)
            gate, up, dhidden = gf[r, :], uf[r, :], df[r, :]
            s = 1.0 / (1.0 + jnp.exp(-gate))
            swish = gate * s
            hid[w, :] = (swish * up).astype(BF16)
            dg[w, :] = (dhidden * up * s * (1.0 + gate * (1.0 - s))).astype(BF16)
            du[w, :] = (dhidden * swish).astype(BF16)

    def transpose(q, src, start, stop):
        for i in range(start, stop):
            lt[q * PANEL:(q + 1) * PANEL, i * 128:(i + 1) * 128] = src[i * 128:(i + 1) * 128, :].T

    def wait_over(a, slots):
        for slot in slots:
            over[a, slot].wait_recv()

    weights[0].wait()
    weights[1].wait()
    wait_over(0, (OWN, LEFT, RIGHT, ACROSS))
    gate_up(0)
    weights[2].wait()
    wait_over(1, (OWN, LEFT, RIGHT, ACROSS))
    backward(0)
    for a in (0, 1):
        relay[a].wait_recv()
        to_across[a, FAR] = message(block(a, FAR), block(a, ACROSS_FAR), z_across)
        to_across[a, FAR].start()
        over[a, FAR] = hand_over(a, FAR)
    for q, src in enumerate((dg, du, hid)):
        transpose(q, src, 0, 2)
    for a in (0, 1):
        to_right[a, ACROSS].wait_recv()
        over[a, ACROSS_LEFT] = hand_over(a, ACROSS_LEFT)
        to_left[a, ACROSS].wait_recv()
        over[a, ACROSS_RIGHT] = hand_over(a, ACROSS_RIGHT)
        to_across[a, FAR].wait_recv()
        over[a, ACROSS_FAR] = hand_over(a, ACROSS_FAR)
        wait_over(a, (FAR, ACROSS_LEFT, ACROSS_RIGHT, ACROSS_FAR))
        if a == 0:
            gate_up(PART)
    backward(PART)
    gather = list(pending)

    def place(z, yr):
        d = ((zl + z) % 2) * 4 + (y + yr) % 4
        return pl.ds(pl.multiple_of(d * PANEL, PANEL), PANEL)

    def grad_gate_up(z, yr):
        @pl.loop(0, 2)
        def _(q):
            r = pl.ds(pl.multiple_of(q * PANEL, PANEL), PANEL)
            pgu[z, yr, r, :] = mm(lt[r, :], xc[0, :, place(z, yr)]).astype(BF16)

    def grad_down(z, yr):
        total = mm(lt[2 * PANEL:, :], xc[1, :, place(z, yr)]).astype(BF16)
        if z:
            pdo[yr] = total
        else:
            wd[:, yr * PANEL:(yr + 1) * PANEL] = total

    class Ring:
        def __init__(self, own, spare, right, left, rows, step):
            self.own, self.spare, self.right, self.left = own, spare, right, left
            self.rows, self.step = rows, step

        def far(self):
            own, spare = self.own, self.spare
            self.far0 = message(own(0, 2), spare(0, 0), self.right)
            self.far1 = message(own(1, 2), spare(0, 1), self.left)
            self.far0.start()
            self.far1.start()

        def near(self):
            own, spare = self.own, self.spare
            self.near1 = message(own(1, 1), spare(1, 1), self.right)
            self.near0 = message(own(0, 3), spare(1, 0), self.left)
            self.near1.start()
            self.near0.start()

        def pass_on(self):
            own, spare = self.own, self.spare
            self.far0.wait_recv()
            add_into(own(0, 1), spare(0, 0), self.rows, self.step)
            self.last0 = message(own(0, 1), spare(2, 0), self.right)
            self.last0.start()
            self.far1.wait_recv()
            add_into(own(1, 3), spare(0, 1), self.rows, self.step)
            self.last1 = message(own(1, 3), spare(2, 1), self.left)
            self.last1.start()

        def finish(self, lane, extra=()):
            (self.near0, self.near1)[lane].wait_recv()
            (self.last0, self.last1)[lane].wait_recv()
            spare = self.spare
            mine = self.own(lane, 0)
            sum_to(mine, (mine, spare(1, lane), spare(2, lane)) + tuple(extra), self.rows, self.step)

    def gate_up_ring(z):
        return Ring(
            lambda lane, yr: pgu.at[z, yr, pl.ds(lane * PANEL, PANEL), :],
            lambda kind, lane: gring.at[z, kind, lane],
            y_right, y_left, PANEL, 64,
        )

    down_ring = Ring(
        lambda lane, yr: wd.at[pl.ds(lane * 256, 256), pl.ds(yr * PANEL, PANEL)],
        lambda kind, lane: dring.at[kind, lane],
        y_right, y_left, 256, 64,
    )

    slot_of = ((OWN, RIGHT, FAR, LEFT), (ACROSS, ACROSS_RIGHT, ACROSS_FAR, ACROSS_LEFT))

    def token_rows(m, slot, cols):
        rows = pl.ds(slot * BLOCK, BLOCK)
        return am.at[rows, cols] if m == 0 else xc.at[1, rows, cols]

    def token_ring(m, z):
        return Ring(
            lambda lane, xr: token_rows(m, slot_of[z][xr], pl.ds(lane * LANE, LANE)),
            lambda kind, lane: mring.at[m, z, kind, lane],
            x_right, x_left, BLOCK, 16,
        )

    gu = [gate_up_ring(0), gate_up_ring(1)]
    tr = {(m, z): token_ring(m, z) for m in (0, 1) for z in (0, 1)}

    transpose(0, dg, 2, 5)
    transpose(1, du, 2, 5)
    grad_gate_up(1, 2)
    gu[1].far()
    transpose(2, hid, 2, 5)
    down_z = {}
    for yr in (2, 1, 3, 0):
        grad_down(1, yr)
        down_z[yr] = message(pdo.at[yr], dz.at[yr], z_next)
        down_z[yr].start()
    grad_gate_up(1, 1)
    grad_gate_up(1, 3)
    gu[1].near()

    @pl.loop(0, 4)
    def _(j):
        cols = pl.ds(pl.multiple_of((1 - c) * HALF + j * PANEL, PANEL), PANEL)
        pgu[0, j, 0:ROWS, :] = mm(hid[...], wd[:, cols]).astype(BF16)

    mixed_over = [message(pgu.at[0, j, pl.ds(0, ROWS), :], sm.at[j], sibling) for j in range(4)]
    for copy in mixed_over:
        copy.start()

    @pl.loop(0, 4)
    def _(j):
        cols = pl.ds(pl.multiple_of(c * HALF + j * PANEL, PANEL), PANEL)
        am[:, pl.ds(pl.multiple_of(j * PANEL, PANEL), PANEL)] = mm(hid[...], wd[:, cols]).astype(BF16)

    grad_gate_up(1, 0)
    for copy in mixed_over:
        wait_send(copy)
    grad_gate_up(0, 2)
    gu[0].far()
    grad_gate_up(0, 1)
    grad_gate_up(0, 3)
    gu[0].near()

    for j in range(4):
        mixed_over[j].wait_recv()
        add_into(am.at[:, pl.ds(j * PANEL, PANEL)], sm.at[j], ROWS, 64)
    pl.semaphore_signal(credit, inc=1, device_id=sibling, device_id_type=MESH)
    for z in (1, 0):
        tr[0, z].far()
        tr[0, z].near()
    gu[1].pass_on()
    for yr in (2, 1, 3, 0):
        grad_down(0, yr)

    for copy in gather:
        wait_send(copy)

    def input_grad(base, j):
        w = pl.ds(pl.multiple_of(base * HALF + j * PANEL, PANEL), PANEL)
        return (mm_nt(dg[...], wg[w, :]) + mm_nt(du[...], wu[w, :])).astype(BF16)

    @pl.loop(0, 4)
    def _(j):
        xc[1, :, pl.ds(pl.multiple_of(HALF + j * PANEL, PANEL), PANEL)] = input_grad(1 - c, j)

    pl.semaphore_wait(credit, 1)
    ig_over = [message(xc.at[1, :, pl.ds(HALF + j * PANEL, PANEL)], sm.at[j], sibling) for j in range(4)]
    for copy in ig_over:
        copy.start()

    @pl.loop(0, 4)
    def _(j):
        xc[1, :, pl.ds(pl.multiple_of(j * PANEL, PANEL), PANEL)] = input_grad(c, j)

    for j in range(4):
        ig_over[j].wait_recv()
        add_into(xc.at[1, :, pl.ds(j * PANEL, PANEL)], sm.at[j], ROWS, 64)
    for z in (1, 0):
        tr[1, z].far()
        tr[1, z].near()
    for z in (1, 0):
        tr[0, z].pass_on()
    grad_gate_up(0, 0)
    gu[0].pass_on()
    for z in (1, 0):
        tr[1, z].pass_on()

    token_z = {}

    def send_across(m):
        for lane in (0, 1):
            tr[m, 1].finish(lane)
        token_z[m] = message(token_rows(m, ACROSS, pl.ds(0, HALF)), mz.at[m], z_across)
        token_z[m].start()

    def down_step(yr):
        down_z[yr].wait_recv()
        add_into(wd.at[:, pl.ds(yr * PANEL, PANEL)], dz.at[yr], PANEL, 64)

    send_across(0)
    down_step(2)
    down_ring.far()
    gu_z = []
    for lane in (0, 1):
        gu[1].finish(lane)
        copy = message(pgu.at[1, 0, pl.ds(lane * PANEL, PANEL), :], gz.at[lane], z_next)
        copy.start()
        gu_z.append(copy)
    send_across(1)
    down_step(1)
    down_step(3)
    down_ring.near()
    down_step(0)
    down_ring.pass_on()

    outs = []
    for m, out in enumerate((mixed_out, ig_out)):
        for lane in (0, 1):
            tr[m, 0].finish(lane)
        token_z[m].wait_recv()
        rows = token_rows(m, OWN, pl.ds(0, HALF))

        @pl.loop(0, 4)
        def _(j, m=m, rows=rows):
            cols = pl.ds(pl.multiple_of(j * PANEL, PANEL), PANEL)
            total = rows[:, cols].astype(F32) + mz[m, :, cols].astype(F32)
            top, bottom = total[:BLOCK // 2], total[BLOCK // 2:]
            fo[m, 0, :, cols] = jnp.where(c == 0, top, bottom).astype(BF16)
            fo[m, 1, :, cols] = jnp.where(c == 0, bottom, top).astype(BF16)

        keep = pltpu.make_async_copy(fo.at[m, 0], out.at[:, mine], local_sem.at[5 + m])
        give = message(fo.at[m, 1], out.at[:, mine], sibling)
        keep.start()
        give.start()
        outs.append((keep, give))

    grads = []
    for lane, out in enumerate((gate_out, up_out)):
        gu_z[lane].wait_recv()
        gu[0].finish(lane, (gz.at[lane],))
        copy = pltpu.make_async_copy(pgu.at[0, 0, pl.ds(lane * PANEL, PANEL), :], out, local_sem.at[7 + lane])
        copy.start()
        grads.append(copy)
    for lane in (0, 1):
        down_ring.finish(lane)
    copy = pltpu.make_async_copy(wd.at[:, pl.ds(0, PANEL)], down_out, local_sem.at[9])
    copy.start()
    grads.append(copy)

    for keep, give in outs:
        keep.wait()
        give.wait_recv()
    for copy in grads:
        copy.wait()
    for copy in pending:
        wait_send(copy)


def on_device(tokens, w_gate, w_up, w_down, cotangent):
    v = lambda *shape: pltpu.VMEM(shape, BF16)
    mixed, input_grad, gate, up, down = pl.pallas_call(
        kernel,
        out_shape=[jax.ShapeDtypeStruct((BLOCK // 2, D), BF16)] * 2
        + [jax.ShapeDtypeStruct((PANEL, PANEL), BF16)] * 3,
        in_specs=[pl.BlockSpec(memory_space=pl.ANY)] * 5,
        out_specs=[pl.BlockSpec(memory_space=pl.ANY)] * 5,
        scratch_shapes=[
            v(D, PANEL), v(D, PANEL), v(PANEL, D),
            v(2, ROWS, D),
            v(ROWS, PANEL), v(ROWS, PANEL), v(ROWS, PANEL),
            v(3 * PANEL, ROWS),
            pltpu.VMEM((PART, PANEL), F32), pltpu.VMEM((PART, PANEL), F32), pltpu.VMEM((PART, PANEL), F32),
            v(ROWS, HALF), v(4, ROWS, PANEL),
            v(2, 4, 2 * PANEL, PANEL), v(4, PANEL, PANEL),
            v(2, 2, 3, 2, BLOCK, LANE), v(2, BLOCK, HALF),
            v(2, 3, 2, PANEL, PANEL), v(2, PANEL, PANEL),
            v(4, PANEL, PANEL), v(3, 2, PANEL // 2, PANEL),
            v(2, 2, BLOCK // 2, HALF), v(2, 2, BLOCK // 2, HALF),
            pltpu.SemaphoreType.DMA((MESSAGES,)),
            pltpu.SemaphoreType.DMA((MESSAGES,)),
            pltpu.SemaphoreType.DMA((10,)),
            pltpu.SemaphoreType.REGULAR,
        ],
        compiler_params=pltpu.CompilerParams(
            collective_id=0, has_side_effects=True, vmem_limit_bytes=63 * 1024 * 1024
        ),
        cost_estimate=pl.CostEstimate(flops=24_200_000_000, bytes_accessed=16_000_000, transcendentals=330_000),
    )(tokens, w_gate, w_up, w_down, cotangent)
    return mixed, input_grad, gate.T, up.T, down


def solution(mesh):
    in_specs = (
        P(("dp", "mp"), None),
        P(None, "mp"),
        P(None, "mp"),
        P("mp", None),
        P(("dp", "mp"), None),
    )
    out_specs = (
        P(("dp", "mp"), None),
        P(("dp", "mp"), None),
        P("dp", "mp"),
        P("dp", "mp"),
        P("mp", "dp"),
    )
    return jax.shard_map(
        on_device, mesh=mesh, in_specs=in_specs, out_specs=out_specs, check_vma=False
    )
```

time: 488 us -> 160 us (0.33)
  waiting for transfers between devices: 400 us -> 0 us
  Pallas kernels: 0 us -> 150 us
  matrix products: 50.9 us -> 0 us
  other arithmetic: 17.8 us -> 0 us
  between operations: 13.9 us -> 0.64 us
  local copies, waits for them, and re-layouts: 4.28 us -> 9.39 us
    reduce_scatter x3 -> x0, waiting for transfers between devices: 284 us -> none  [the longest x1 113 us: on_device(): lax.psum_scatter(jnp.concatenate([contract_rows(gathered, dgate), contrac...]
    pallas_call x0 -> x1, Pallas kernels: none -> 150 us  [on_device(): pl.pallas_call(kernel, out_shape=[jax.ShapeDtypeStruct((BLOCK // 2, D), B...]
    all_gather x2 -> x0, waiting for transfers between devices: 115 us -> none  [the longest x1 65.3 us: on_device(): gathered = lax.all_gather(tokens, 'mp', axis=0, tiled=True)]
    dot_general x9 -> x0, matrix products: 50.9 us -> none  [the longest x3 18.2 us: contract_cols(): lax.dot_general(left, right, (((1,), (1,)), ((), ())), preferred_element_...]
    concatenate x1 -> x0, other arithmetic: 17.8 us -> none  [on_device(): jnp.concatenate([contract_rows(gathered, dgate), contract_rows(gathered,...]
    unnamed x14 -> x5, local copies, waits for them, and re-layouts: 2.03 us -> 9.39 us
  transfers between devices with their start and end apart: 5 -> 0, of which waited for: 5 -> 0; matrix products, arithmetic and copies ran while one was open for 7% -> 0% of each run, Pallas kernels for 0% -> 0%
where the time goes in v1:
time: 160 us
  Pallas kernels  150 us (94%)
  local copies, waits for them, and re-layouts  9.39 us (6%)
    pallas_call x1, Pallas kernels, on_device(): pl.pallas_call(kernel, out_shape=[jax.ShapeDtypeStruct((BLOCK // 2, D), B...  150 us
    unnamed x5, local copies, waits for them, and re-layouts  9.39 us

profile of v1, /device:TPU:1, one launch (start us, length us, event | category | flops | bytes accessed | tf_op | source)
XLA Modules:
  0.0 159.8 jit_solution(12797467304961609574)
XLA Ops:
  0.6 149.8 %shard_map.92 = (bf16[40,4096]{1,0:T(8,128)(2,1)}, bf16[40,4096]{1,0:T(8,128)(2,1)}, bf16[512,512]{1,0:T(8,128)(2,1)}, bf16[512,512]{1,0:T(8,128)(2,1)}, bf16[512,512]{1,0:T(8,128)(2,1)}) custom-call(bf16[40,4096]{1,0:T(8,128)(2,1)} %tok_hbm.1, bf16[4096,512]{1,0:T(8,128)(2,1)} %wg_hbm.1, bf16[4096,512]{1,0:T(8,128)(2,1)} %wu_hbm.1, ...), custom_call_target="tpu_custom_call" | custom-call | flops 24199999488 | bytes 16000000 | tf_op jit(solution)/shard_map/pallas_call | solution.py:456
  150.4 2.0 %copy.10 = bf16[512,512]{1,0:T(8,128)(2,1)} copy(bf16[512,512]{0,1:T(8,128)(2,1)} %bitcast.3) | data formatting | bytes 1048576
  152.5 2.0 %copy.11 = bf16[512,512]{1,0:T(8,128)(2,1)} copy(bf16[512,512]{0,1:T(8,128)(2,1)} %bitcast.2) | data formatting | bytes 1048576
  154.5 1.7 %copy.15 = bf16[40,4096]{1,0:T(8,128)(2,1)} copy(bf16[40,4096]{1,0:T(8,128)(2,1)} %get-tuple-element.25) | data formatting | bytes 655360
  156.2 1.7 %copy.16 = bf16[40,4096]{1,0:T(8,128)(2,1)} copy(bf16[40,4096]{1,0:T(8,128)(2,1)} %get-tuple-element.26) | data formatting | bytes 655360
  157.9 1.9 %copy.17 = bf16[512,512]{1,0:T(8,128)(2,1)} copy(bf16[512,512]{1,0:T(8,128)(2,1)} %get-tuple-element.29) | data formatting | bytes 1048576

commit v2 on v1

--- a/solution.py
+++ b/solution.py
@@ -91,8 +91,6 @@
     own_rows = [pltpu.make_async_copy(inputs[a].at[:, mine], t_in.at[c, a], local_sem.at[3 + a]) for a in (0, 1)]
     for copy in own_rows:
         copy.start()
-    for copy in weights:
-        copy.start()
 
     barrier = pltpu.get_barrier_semaphore()
     partners = (x_right, x_left, z_across, sibling, y_right, y_left, z_next)
@@ -112,6 +110,7 @@
         copy.start()
         return copy
 
+    parts = [pl.ds(pl.multiple_of(c * HALF + i * LANE, LANE), LANE) for i in (0, 1)]
     to_right, to_left, to_across, relay, over = {}, {}, {}, {}, {}
     for a in (0, 1):
         own_rows[a].wait()
@@ -123,12 +122,21 @@
             both = jnp.concatenate([t_in[0, a, :, cols].astype(F32), t_in[1, a, :, cols].astype(F32)], axis=0)
             xc[a, 0:BLOCK, pl.ds(pl.multiple_of(c * HALF + j * PANEL, PANEL), PANEL)] = both.astype(BF16)
 
-        to_right[a, OWN] = message(block(a, OWN), block(a, LEFT), x_right)
-        to_left[a, OWN] = message(block(a, OWN), block(a, RIGHT), x_left)
         to_across[a, OWN] = message(block(a, OWN), block(a, ACROSS), z_across)
-        for copy in (to_right[a, OWN], to_left[a, OWN], to_across[a, OWN]):
-            copy.start()
+        if a == 0:
+            to_right[0, OWN] = message(block(0, OWN), block(0, LEFT), x_right)
+            to_right[0, OWN].start()
+        else:
+            to_left[1, OWN] = message(block(1, OWN), block(1, RIGHT), x_left)
+            to_left[1, OWN].start()
+            to_right[1, OWN] = [message(block(1, OWN, cols), block(1, LEFT, cols), x_right) for cols in parts]
+            to_left[0, OWN] = [message(block(0, OWN, cols), block(0, RIGHT, cols), x_left) for cols in parts]
+            to_right[1, OWN][0].start()
+            to_left[0, OWN][0].start()
+        to_across[a, OWN].start()
         over[a, OWN] = hand_over(a, OWN)
+    for copy in weights:
+        copy.start()
 
     def relay_far(a):
         if a == 0:
@@ -137,94 +145,138 @@
             relay[a] = message(block(a, RIGHT), block(a, FAR), x_left)
         relay[a].start()
 
-    for a in (0, 1):
-        first, second = (to_right, to_left) if a == 0 else (to_left, to_right)
-        first[a, OWN].wait_recv()
-        relay_far(a)
-        over[a, LEFT if a == 0 else RIGHT] = hand_over(a, LEFT if a == 0 else RIGHT)
+    def from_across(a):
         to_across[a, OWN].wait_recv()
         to_right[a, ACROSS] = message(block(a, ACROSS), block(a, ACROSS_LEFT), x_right)
         to_left[a, ACROSS] = message(block(a, ACROSS), block(a, ACROSS_RIGHT), x_left)
         to_right[a, ACROSS].start()
         to_left[a, ACROSS].start()
         over[a, ACROSS] = hand_over(a, ACROSS)
-        second[a, OWN].wait_recv()
-        over[a, RIGHT if a == 0 else LEFT] = hand_over(a, RIGHT if a == 0 else LEFT)
-
-    def gate_up(r0):
+
+    def from_far(a):
+        relay[a].wait_recv()
+        to_across[a, FAR] = message(block(a, FAR), block(a, ACROSS_FAR), z_across)
+        to_across[a, FAR].start()
+        over[a, FAR] = hand_over(a, FAR)
+
+    def arrived(copy, a, slot):
+        copy.wait_recv()
+        over[a, slot] = hand_over(a, slot)
+
+    def wait_over(a, slots):
+        for slot in slots:
+            over[a, slot].wait_recv()
+
+    def columns(k):
+        return pl.ds(pl.multiple_of((c * 2 + k) % 4 * 1024, 1024), 1024)
+
+    def gate_up(r0, slots):
         gf[...] = jnp.zeros_like(gf)
         uf[...] = jnp.zeros_like(uf)
 
-        @pl.loop(0, 4)
-        def _(k):
-            ks = pl.ds(pl.multiple_of(k * 1024, 1024), 1024)
+        def step(k):
+            ks = columns(k)
             rows = xc[0, r0:r0 + PART, ks]
             gf[...] += mm(rows, wg[ks, :])
             uf[...] += mm(rows, wu[ks, :])
 
-    def backward(r0):
-        df[...] = jnp.zeros_like(df)
-
-        @pl.loop(0, 4)
-        def _(k):
-            ks = pl.ds(pl.multiple_of(k * 1024, 1024), 1024)
-            df[...] += mm_nt(xc[1, r0:r0 + PART, ks], wd[:, ks])
+        pl.loop(0, 2)(step)
+        wait_over(0, slots)
+        pl.loop(2, 4)(step)
 
         @pl.loop(0, PART // 32)
         def _(i):
             r = pl.ds(pl.multiple_of(i * 32, 32), 32)
             w = pl.ds(pl.multiple_of(r0 + i * 32, 32), 32)
-            gate, up, dhidden = gf[r, :], uf[r, :], df[r, :]
+            gate, up = gf[r, :], uf[r, :]
             s = 1.0 / (1.0 + jnp.exp(-gate))
             swish = gate * s
             hid[w, :] = (swish * up).astype(BF16)
-            dg[w, :] = (dhidden * up * s * (1.0 + gate * (1.0 - s))).astype(BF16)
-            du[w, :] = (dhidden * swish).astype(BF16)
+            gf[r, :] = up * s * (1.0 + gate * (1.0 - s))
+            uf[r, :] = swish
+
+    def backward(r0, slots):
+        df[...] = jnp.zeros_like(df)
+
+        def step(k):
+            ks = columns(k)
+            df[...] += mm_nt(xc[1, r0:r0 + PART, ks], wd[:, ks])
+
+        pl.loop(0, 2)(step)
+        wait_over(1, slots)
+        pl.loop(2, 4)(step)
+
+        @pl.loop(0, PART // 32)
+        def _(i):
+            r = pl.ds(pl.multiple_of(i * 32, 32), 32)
+            w = pl.ds(pl.multiple_of(r0 + i * 32, 32), 32)
+            dhidden = df[r, :]
+            dg[w, :] = (dhidden * gf[r, :]).astype(BF16)
+            du[w, :] = (dhidden * uf[r, :]).astype(BF16)
+
+    def mixed_part(r0):
+        @pl.loop(0, 4)
+        def _(j):
+            cols = pl.ds(pl.multiple_of((1 - c) * HALF + j * PANEL, PANEL), PANEL)
+            pgu[0, j, r0:r0 + PART, :] = mm(hid[r0:r0 + PART, :], wd[:, cols]).astype(BF16)
+
+        @pl.loop(0, 4)
+        def _(j):
+            cols = pl.ds(pl.multiple_of(c * HALF + j * PANEL, PANEL), PANEL)
+            total = mm(hid[r0:r0 + PART, :], wd[:, cols]).astype(BF16)
+            am[r0:r0 + PART, pl.ds(pl.multiple_of(j * PANEL, PANEL), PANEL)] = total
 
     def transpose(q, src, start, stop):
         for i in range(start, stop):
             lt[q * PANEL:(q + 1) * PANEL, i * 128:(i + 1) * 128] = src[i * 128:(i + 1) * 128, :].T
 
-    def wait_over(a, slots):
-        for slot in slots:
-            over[a, slot].wait_recv()
-
+    to_right[0, OWN].wait_recv()
+    relay_far(0)
+    to_right[1, OWN][1].start()
+    to_left[1, OWN].wait_recv()
+    relay_far(1)
+    to_left[0, OWN][1].start()
+    over[0, LEFT] = hand_over(0, LEFT)
+    over[1, RIGHT] = hand_over(1, RIGHT)
+    from_across(0)
+    from_across(1)
+    from_far(0)
+    from_far(1)
+    for a, slot, halves in ((0, RIGHT, to_left[0, OWN]), (1, LEFT, to_right[1, OWN])):
+        halves[0].wait_recv()
+        arrived(halves[1], a, slot)
+    near = (OWN, LEFT, RIGHT, ACROSS)
+    distant = (FAR, ACROSS_LEFT, ACROSS_RIGHT, ACROSS_FAR)
     weights[0].wait()
     weights[1].wait()
-    wait_over(0, (OWN, LEFT, RIGHT, ACROSS))
-    gate_up(0)
+    gate_up(0, near)
     weights[2].wait()
-    wait_over(1, (OWN, LEFT, RIGHT, ACROSS))
-    backward(0)
-    for a in (0, 1):
-        relay[a].wait_recv()
-        to_across[a, FAR] = message(block(a, FAR), block(a, ACROSS_FAR), z_across)
-        to_across[a, FAR].start()
-        over[a, FAR] = hand_over(a, FAR)
+    backward(0, near)
     for q, src in enumerate((dg, du, hid)):
         transpose(q, src, 0, 2)
+    mixed_part(0)
     for a in (0, 1):
-        to_right[a, ACROSS].wait_recv()
-        over[a, ACROSS_LEFT] = hand_over(a, ACROSS_LEFT)
-        to_left[a, ACROSS].wait_recv()
-        over[a, ACROSS_RIGHT] = hand_over(a, ACROSS_RIGHT)
-        to_across[a, FAR].wait_recv()
-        over[a, ACROSS_FAR] = hand_over(a, ACROSS_FAR)
-        wait_over(a, (FAR, ACROSS_LEFT, ACROSS_RIGHT, ACROSS_FAR))
+        arrived(to_left[a, ACROSS], a, ACROSS_RIGHT)
+        arrived(to_right[a, ACROSS], a, ACROSS_LEFT)
+        arrived(to_across[a, FAR], a, ACROSS_FAR)
         if a == 0:
-            gate_up(PART)
-    backward(PART)
+            gate_up(PART, distant)
+            transpose(2, hid, 2, 5)
+    backward(PART, distant)
     gather = list(pending)
 
     def place(z, yr):
         d = ((zl + z) % 2) * 4 + (y + yr) % 4
         return pl.ds(pl.multiple_of(d * PANEL, PANEL), PANEL)
 
+    def grad_lane(z, yr, lane):
+        r = pl.ds(pl.multiple_of(lane * PANEL, PANEL), PANEL)
+        pgu[z, yr, r, :] = mm(lt[r, :], xc[0, :, place(z, yr)]).astype(BF16)
+
     def grad_gate_up(z, yr):
         @pl.loop(0, 2)
         def _(q):
-            r = pl.ds(pl.multiple_of(q * PANEL, PANEL), PANEL)
-            pgu[z, yr, r, :] = mm(lt[r, :], xc[0, :, place(z, yr)]).astype(BF16)
+            grad_lane(z, yr, q)
 
     def grad_down(z, yr):
         total = mm(lt[2 * PANEL:, :], xc[1, :, place(z, yr)]).astype(BF16)
@@ -238,12 +290,14 @@
             self.own, self.spare, self.right, self.left = own, spare, right, left
             self.rows, self.step = rows, step
 
+        def far_lane(self, lane):
+            copy = message(self.own(lane, 2), self.spare(0, lane), (self.right, self.left)[lane])
+            setattr(self, ("far0", "far1")[lane], copy)
+            copy.start()
+
         def far(self):
-            own, spare = self.own, self.spare
-            self.far0 = message(own(0, 2), spare(0, 0), self.right)
-            self.far1 = message(own(1, 2), spare(0, 1), self.left)
-            self.far0.start()
-            self.far1.start()
+            self.far_lane(0)
+            self.far_lane(1)
 
         def near(self):
             own, spare = self.own, self.spare
@@ -300,10 +354,11 @@
     tr = {(m, z): token_ring(m, z) for m in (0, 1) for z in (0, 1)}
 
     transpose(0, dg, 2, 5)
+    grad_lane(1, 2, 0)
+    gu[1].far_lane(0)
     transpose(1, du, 2, 5)
-    grad_gate_up(1, 2)
-    gu[1].far()
-    transpose(2, hid, 2, 5)
+    grad_lane(1, 2, 1)
+    gu[1].far_lane(1)
     down_z = {}
     for yr in (2, 1, 3, 0):
         grad_down(1, yr)
@@ -312,22 +367,18 @@
     grad_gate_up(1, 1)
     grad_gate_up(1, 3)
     gu[1].near()
-
-    @pl.loop(0, 4)
-    def _(j):
-        cols = pl.ds(pl.multiple_of((1 - c) * HALF + j * PANEL, PANEL), PANEL)
-        pgu[0, j, 0:ROWS, :] = mm(hid[...], wd[:, cols]).astype(BF16)
-
+    mixed_part(PART)
     mixed_over = [message(pgu.at[0, j, pl.ds(0, ROWS), :], sm.at[j], sibling) for j in range(4)]
     for copy in mixed_over:
         copy.start()
-
-    @pl.loop(0, 4)
-    def _(j):
-        cols = pl.ds(pl.multiple_of(c * HALF + j * PANEL, PANEL), PANEL)
-        am[:, pl.ds(pl.multiple_of(j * PANEL, PANEL), PANEL)] = mm(hid[...], wd[:, cols]).astype(BF16)
-
-    grad_gate_up(1, 0)
+    for yr in (2, 1, 3, 0):
+        grad_down(0, yr)
+    for j in range(4):
+        mixed_over[j].wait_recv()
+        add_into(am.at[:, pl.ds(j * PANEL, PANEL)], sm.at[j], ROWS, 64)
+    pl.semaphore_signal(credit, inc=1, device_id=sibling, device_id_type=MESH)
+    tr[0, 1].far()
+    tr[0, 1].near()
     for copy in mixed_over:
         wait_send(copy)
     grad_gate_up(0, 2)
@@ -336,17 +387,6 @@
     grad_gate_up(0, 3)
     gu[0].near()
 
-    for j in range(4):
-        mixed_over[j].wait_recv()
-        add_into(am.at[:, pl.ds(j * PANEL, PANEL)], sm.at[j], ROWS, 64)
-    pl.semaphore_signal(credit, inc=1, device_id=sibling, device_id_type=MESH)
-    for z in (1, 0):
-        tr[0, z].far()
-        tr[0, z].near()
-    gu[1].pass_on()
-    for yr in (2, 1, 3, 0):
-        grad_down(0, yr)
-
     for copy in gather:
         wait_send(copy)
 
@@ -367,18 +407,18 @@
     def _(j):
         xc[1, :, pl.ds(pl.multiple_of(j * PANEL, PANEL), PANEL)] = input_grad(c, j)
 
+    tr[0, 1].pass_on()
     for j in range(4):
         ig_over[j].wait_recv()
         add_into(xc.at[1, :, pl.ds(j * PANEL, PANEL)], sm.at[j], ROWS, 64)
-    for z in (1, 0):
-        tr[1, z].far()
-        tr[1, z].near()
-    for z in (1, 0):
-        tr[0, z].pass_on()
+    tr[1, 1].far()
+    tr[1, 1].near()
+    for m in (0, 1):
+        tr[m, 0].far()
+        tr[m, 0].near()
+    gu[1].pass_on()
+    grad_gate_up(1, 0)
     grad_gate_up(0, 0)
-    gu[0].pass_on()
-    for z in (1, 0):
-        tr[1, z].pass_on()
 
     token_z = {}
 
@@ -392,20 +432,24 @@
         down_z[yr].wait_recv()
         add_into(wd.at[:, pl.ds(yr * PANEL, PANEL)], dz.at[yr], PANEL, 64)
 
-    send_across(0)
     down_step(2)
     down_ring.far()
+    send_across(0)
+    tr[1, 1].pass_on()
+    down_step(1)
+    down_step(3)
+    down_ring.near()
+    gu[0].pass_on()
+    send_across(1)
+    for m in (0, 1):
+        tr[m, 0].pass_on()
+    down_step(0)
     gu_z = []
     for lane in (0, 1):
         gu[1].finish(lane)
         copy = message(pgu.at[1, 0, pl.ds(lane * PANEL, PANEL), :], gz.at[lane], z_next)
         copy.start()
         gu_z.append(copy)
-    send_across(1)
-    down_step(1)
-    down_step(3)
-    down_ring.near()
-    down_step(0)
     down_ring.pass_on()
 
     outs = []
@@ -433,7 +477,8 @@
     for lane, out in enumerate((gate_out, up_out)):
         gu_z[lane].wait_recv()
         gu[0].finish(lane, (gz.at[lane],))
-        copy = pltpu.make_async_copy(pgu.at[0, 0, pl.ds(lane * PANEL, PANEL), :], out, local_sem.at[7 + lane])
+        gring[0, 0, lane] = pgu[0, 0, lane * PANEL:(lane + 1) * PANEL, :].T
+        copy = pltpu.make_async_copy(gring.at[0, 0, lane], out, local_sem.at[7 + lane])
         copy.start()
         grads.append(copy)
     for lane in (0, 1):
@@ -451,12 +496,25 @@
         wait_send(copy)
 
 
+def arrange(*refs):
+    sources, results, held, sem = refs[:5], refs[5:10], refs[10:15], refs[15]
+    ins = [pltpu.make_async_copy(sources[n], held[n], sem.at[n]) for n in range(5)]
+    outs = [pltpu.make_async_copy(held[n], results[n], sem.at[5 + n]) for n in range(5)]
+    for copy in ins:
+        copy.start()
+    for n in range(5):
+        ins[n].wait()
+        outs[n].start()
+    for copy in outs:
+        copy.wait()
+
+
 def on_device(tokens, w_gate, w_up, w_down, cotangent):
     v = lambda *shape: pltpu.VMEM(shape, BF16)
-    mixed, input_grad, gate, up, down = pl.pallas_call(
+    shapes = [jax.ShapeDtypeStruct((BLOCK // 2, D), BF16)] * 2 + [jax.ShapeDtypeStruct((PANEL, PANEL), BF16)] * 3
+    results = pl.pallas_call(
         kernel,
-        out_shape=[jax.ShapeDtypeStruct((BLOCK // 2, D), BF16)] * 2
-        + [jax.ShapeDtypeStruct((PANEL, PANEL), BF16)] * 3,
+        out_shape=shapes,
         in_specs=[pl.BlockSpec(memory_space=pl.ANY)] * 5,
         out_specs=[pl.BlockSpec(memory_space=pl.ANY)] * 5,
         scratch_shapes=[
@@ -481,7 +539,14 @@
         ),
         cost_estimate=pl.CostEstimate(flops=24_200_000_000, bytes_accessed=16_000_000, transcendentals=330_000),
     )(tokens, w_gate, w_up, w_down, cotangent)
-    return mixed, input_grad, gate.T, up.T, down
+    return pl.pallas_call(
+        arrange,
+        out_shape=shapes,
+        in_specs=[pl.BlockSpec(memory_space=pl.ANY)] * 5,
+        out_specs=[pl.BlockSpec(memory_space=pl.ANY)] * 5,
+        scratch_shapes=[pltpu.VMEM(shape.shape, BF16) for shape in shapes] + [pltpu.SemaphoreType.DMA((10,))],
+        compiler_params=pltpu.CompilerParams(vmem_limit_bytes=60 * 1024 * 1024),
+    )(*results)
 
 
 def solution(mesh):

time: 160 us -> 144 us (0.900)
  local copies, waits for them, and re-layouts: 9.39 us -> 0 us
  Pallas kernels: 150 us -> 143 us
    unnamed x5 -> x0, local copies, waits for them, and re-layouts: 9.39 us -> none
    pallas_call x1 -> x2, Pallas kernels: 150 us -> 143 us  [the longest x1 141 us: on_device(): pl.pallas_call(kernel, out_shape=shapes, in_specs=[pl.BlockSpec(memory_sp...]
where the time goes in v2:
time: 144 us
  Pallas kernels  143 us (99%)
    pallas_call x1, Pallas kernels, on_device(): pl.pallas_call(kernel, out_shape=shapes, in_specs=[pl.BlockSpec(memory_sp...  141 us

profile of v2, /device:TPU:1, one launch (start us, length us, event | category | flops | bytes accessed | tf_op | source)
XLA Modules:
  0.0 143.8 jit_solution(15485745665187386745)
XLA Ops:
  0.6 140.7 %shard_map.92 = (bf16[40,4096]{1,0:T(8,128)(2,1)}, bf16[40,4096]{1,0:T(8,128)(2,1)}, bf16[512,512]{1,0:T(8,128)(2,1)}, bf16[512,512]{1,0:T(8,128)(2,1)}, bf16[512,512]{1,0:T(8,128)(2,1)}) custom-call(bf16[40,4096]{1,0:T(8,128)(2,1)} %tok_hbm.1, bf16[4096,512]{1,0:T(8,128)(2,1)} %wg_hbm.1, bf16[4096,512]{1,0:T(8,128)(2,1)} %wu_hbm.1, ...), custom_call_target="tpu_custom_call" | custom-call | flops 24199999488 | bytes 16000000 | tf_op jit(solution)/shard_map/pallas_call | solution.py:515
  141.3 2.5 %shard_map.93 = (bf16[40,4096]{1,0:T(8,128)(2,1)}, bf16[40,4096]{1,0:T(8,128)(2,1)}, bf16[512,512]{1,0:T(8,128)(2,1)}, bf16[512,512]{1,0:T(8,128)(2,1)}, bf16[512,512]{1,0:T(8,128)(2,1)}) custom-call(bf16[40,4096]{1,0:T(8,128)(2,1)} %get-tuple-element.10.refs_0_, bf16[40,4096]{1,0:T(8,128)(2,1)} %get-tuple-element.11.refs_1_, ...), custom_call_target="tpu_custom_call" | custom-call | tf_op jit(solution)/shard_map/pallas_call | solution.py:542

commit v3 on v2

--- a/solution.py
+++ b/solution.py
@@ -15,7 +15,8 @@
 ROWS = 640
 BLOCK = 80
 PART = 320
-MESSAGES = 110
+MESSAGES = 160
+QROWS = PANEL // 2
 
 OWN, LEFT, RIGHT, ACROSS, FAR, ACROSS_LEFT, ACROSS_RIGHT, ACROSS_FAR = range(8)
 
@@ -48,8 +49,8 @@
 def kernel(
     tok_hbm, wg_hbm, wu_hbm, wd_hbm, cot_hbm,
     mixed_out, ig_out, gate_out, up_out, down_out,
-    wg, wu, wd, xc, hid, dg, du, lt, gf, uf, df, am, sm, pgu, pdo,
-    mring, mz, gring, gz, dz, dring, t_in, fo,
+    wg, wu, wd, xc, hid, dg, du, lt, gf, uf, df, am, mb, sm, pdo,
+    mring, mz, ry, lty, acc, gzs, gz, fin, dz, dbz, dring, t_in, fo,
     send_sem, recv_sem, local_sem, credit,
 ):
     dp, mp = lax.axis_index("dp"), lax.axis_index("mp")
@@ -61,6 +62,7 @@
     sibling = (dp, zh * 8 + x * 2 + (1 - c))
     y_right = (zl * 4 + (y + 1) % 4, mp)
     y_left = (zl * 4 + (y + 3) % 4, mp)
+    y_far = (zl * 4 + (y + 2) % 4, mp)
     z_next = ((1 - zl) * 4 + y, mp)
     mine = pl.ds(pl.multiple_of(c * HALF, HALF), HALF)
     other = pl.ds(pl.multiple_of((1 - c) * HALF, HALF), HALF)
@@ -93,7 +95,7 @@
         copy.start()
 
     barrier = pltpu.get_barrier_semaphore()
-    partners = (x_right, x_left, z_across, sibling, y_right, y_left, z_next)
+    partners = (x_right, x_left, z_across, sibling, y_right, y_left, y_far, z_next)
     for device in partners:
         pl.semaphore_signal(barrier, inc=1, device_id=device, device_id_type=MESH)
     pl.semaphore_wait(barrier, len(partners))
@@ -105,9 +107,21 @@
     def block(a, slot, cols=mine):
         return xc.at[a, pl.ds(slot * BLOCK, BLOCK), cols]
 
+    r_half = pl.ds(pl.multiple_of(c * PANEL, PANEL), PANEL)
+    r_sent = {}
+
+    def send_columns(slot):
+        rows = pl.ds(slot * BLOCK, BLOCK)
+        for yr, device in ((1, y_right), (3, y_left), (2, y_far)):
+            cols = pl.ds(pl.multiple_of(c * HALF + (y + yr) % 4 * PANEL, PANEL), PANEL)
+            r_sent[yr, slot] = message(xc.at[0, rows, cols], ry.at[3 - yr, rows, r_half], device)
+            r_sent[yr, slot].start()
+
     def hand_over(a, slot):
         copy = message(block(a, slot), block(a, slot), sibling)
         copy.start()
+        if a == 0:
+            send_columns(slot)
         return copy
 
     parts = [pl.ds(pl.multiple_of(c * HALF + i * LANE, LANE), LANE) for i in (0, 1)]
@@ -218,7 +232,7 @@
         @pl.loop(0, 4)
         def _(j):
             cols = pl.ds(pl.multiple_of((1 - c) * HALF + j * PANEL, PANEL), PANEL)
-            pgu[0, j, r0:r0 + PART, :] = mm(hid[r0:r0 + PART, :], wd[:, cols]).astype(BF16)
+            mb[j, r0:r0 + PART, :] = mm(hid[r0:r0 + PART, :], wd[:, cols]).astype(BF16)
 
         @pl.loop(0, 4)
         def _(j):
@@ -254,7 +268,6 @@
     backward(0, near)
     for q, src in enumerate((dg, du, hid)):
         transpose(q, src, 0, 2)
-    mixed_part(0)
     for a in (0, 1):
         arrived(to_left[a, ACROSS], a, ACROSS_RIGHT)
         arrived(to_right[a, ACROSS], a, ACROSS_LEFT)
@@ -262,6 +275,7 @@
         if a == 0:
             gate_up(PART, distant)
             transpose(2, hid, 2, 5)
+            mixed_part(0)
     backward(PART, distant)
     gather = list(pending)
 
@@ -269,14 +283,14 @@
         d = ((zl + z) % 2) * 4 + (y + yr) % 4
         return pl.ds(pl.multiple_of(d * PANEL, PANEL), PANEL)
 
-    def grad_lane(z, yr, lane):
-        r = pl.ds(pl.multiple_of(lane * PANEL, PANEL), PANEL)
-        pgu[z, yr, r, :] = mm(lt[r, :], xc[0, :, place(z, yr)]).astype(BF16)
-
-    def grad_gate_up(z, yr):
-        @pl.loop(0, 2)
-        def _(q):
-            grad_lane(z, yr, q)
+    def grad_term(z, source, rows):
+        if source < 0:
+            return mm(lt[rows, :], xc[0, :, place(z, 0)])
+        cols = pl.ds(pl.multiple_of((zl + z) % 2 * PANEL, PANEL), PANEL)
+        return mm(lty[source, rows, :], ry[source, :, cols])
+
+    def quarter(lane, part):
+        return pl.ds(lane * PANEL + part * QROWS, QROWS)
 
     def grad_down(z, yr):
         total = mm(lt[2 * PANEL:, :], xc[1, :, place(z, yr)]).astype(BF16)
@@ -324,18 +338,17 @@
             mine = self.own(lane, 0)
             sum_to(mine, (mine, spare(1, lane), spare(2, lane)) + tuple(extra), self.rows, self.step)
 
-    def gate_up_ring(z):
-        return Ring(
-            lambda lane, yr: pgu.at[z, yr, pl.ds(lane * PANEL, PANEL), :],
-            lambda kind, lane: gring.at[z, kind, lane],
-            y_right, y_left, PANEL, 64,
-        )
-
-    down_ring = Ring(
-        lambda lane, yr: wd.at[pl.ds(lane * 256, 256), pl.ds(yr * PANEL, PANEL)],
-        lambda kind, lane: dring.at[kind, lane],
-        y_right, y_left, 256, 64,
-    )
+    def down_ring(n, own):
+        return Ring(own, lambda kind, lane: dring.at[n, kind, lane], y_right, y_left, QROWS // 2, 64)
+
+    def lower(lane):
+        return pl.ds(QROWS + lane * (QROWS // 2), QROWS // 2)
+
+    down_a = down_ring(0, lambda lane, yr: wd.at[pl.ds(lane * (QROWS // 2), QROWS // 2), pl.ds(yr * PANEL, PANEL)])
+    down_b = [
+        down_ring(1, lambda lane, yr: wd.at[lower(lane), pl.ds(yr * PANEL, PANEL)]),
+        down_ring(2, lambda lane, yr: pdo.at[yr, lower(lane), :]),
+    ]
 
     slot_of = ((OWN, RIGHT, FAR, LEFT), (ACROSS, ACROSS_RIGHT, ACROSS_FAR, ACROSS_LEFT))
 
@@ -350,25 +363,26 @@
             x_right, x_left, BLOCK, 16,
         )
 
-    gu = [gate_up_ring(0), gate_up_ring(1)]
     tr = {(m, z): token_ring(m, z) for m in (0, 1) for z in (0, 1)}
 
+    def half(ref, lane):
+        return ref.at[pl.ds(lane * PANEL, PANEL), :]
+
+    l_right = [message(half(lt, lane), half(lty.at[2], lane), y_right) for lane in (0, 1)]
+    l_left = [message(half(lt, lane), half(lty.at[0], lane), y_left) for lane in (0, 1)]
     transpose(0, dg, 2, 5)
-    grad_lane(1, 2, 0)
-    gu[1].far_lane(0)
+    l_right[0].start()
     transpose(1, du, 2, 5)
-    grad_lane(1, 2, 1)
-    gu[1].far_lane(1)
+    l_left[1].start()
+    l_right[1].start()
+    l_left[0].start()
     down_z = {}
     for yr in (2, 1, 3, 0):
         grad_down(1, yr)
-        down_z[yr] = message(pdo.at[yr], dz.at[yr], z_next)
+        down_z[yr] = message(pdo.at[yr, pl.ds(0, QROWS), :], dz.at[yr], z_next)
         down_z[yr].start()
-    grad_gate_up(1, 1)
-    grad_gate_up(1, 3)
-    gu[1].near()
     mixed_part(PART)
-    mixed_over = [message(pgu.at[0, j, pl.ds(0, ROWS), :], sm.at[j], sibling) for j in range(4)]
+    mixed_over = [message(mb.at[j], sm.at[j], sibling) for j in range(4)]
     for copy in mixed_over:
         copy.start()
     for yr in (2, 1, 3, 0):
@@ -379,14 +393,6 @@
     pl.semaphore_signal(credit, inc=1, device_id=sibling, device_id_type=MESH)
     tr[0, 1].far()
     tr[0, 1].near()
-    for copy in mixed_over:
-        wait_send(copy)
-    grad_gate_up(0, 2)
-    gu[0].far()
-    grad_gate_up(0, 1)
-    grad_gate_up(0, 3)
-    gu[0].near()
-
     for copy in gather:
         wait_send(copy)
 
@@ -407,18 +413,35 @@
     def _(j):
         xc[1, :, pl.ds(pl.multiple_of(j * PANEL, PANEL), PANEL)] = input_grad(c, j)
 
+    l_far = {}
+    for lane, source, device in ((0, 2, y_right), (1, 0, y_left)):
+        (l_right, l_left)[lane][lane].wait_recv()
+        for part in (0, 1):
+            rows = quarter(lane, part)
+            l_far[lane, part] = message(lty.at[source, rows, :], lty.at[1, rows, :], device)
+            l_far[lane, part].start()
     tr[0, 1].pass_on()
     for j in range(4):
         ig_over[j].wait_recv()
         add_into(xc.at[1, :, pl.ds(j * PANEL, PANEL)], sm.at[j], ROWS, 64)
     tr[1, 1].far()
     tr[1, 1].near()
-    for m in (0, 1):
-        tr[m, 0].far()
-        tr[m, 0].near()
-    gu[1].pass_on()
-    grad_gate_up(1, 0)
-    grad_gate_up(0, 0)
+    down_b[1].far()
+    down_b[1].near()
+    r_over = []
+    for source in (0, 2, 1):
+        for slot in range(8):
+            r_sent[3 - source, slot].wait_recv()
+        columns_held = ry.at[source, :, r_half]
+        copy = message(columns_held, columns_held, sibling)
+        copy.start()
+        r_over.append(copy)
+
+    def accumulate(source, rows):
+        acc[rows, :] = grad_term(1, source, rows) if source < 0 else acc[rows, :] + grad_term(1, source, rows)
+
+    for lane in (0, 1):
+        accumulate(-1, pl.ds(lane * PANEL, PANEL))
 
     token_z = {}
 
@@ -430,27 +453,48 @@
 
     def down_step(yr):
         down_z[yr].wait_recv()
-        add_into(wd.at[:, pl.ds(yr * PANEL, PANEL)], dz.at[yr], PANEL, 64)
-
-    down_step(2)
-    down_ring.far()
+        add_into(wd.at[pl.ds(0, QROWS), pl.ds(yr * PANEL, PANEL)], dz.at[yr], QROWS, 64)
+
     send_across(0)
     tr[1, 1].pass_on()
-    down_step(1)
-    down_step(3)
-    down_ring.near()
-    gu[0].pass_on()
+    for m in (0, 1):
+        tr[m, 0].far()
+        tr[m, 0].near()
+    for copy in r_over:
+        copy.wait_recv()
+    l_left[0].wait_recv()
+    l_right[1].wait_recv()
+    for source in (0, 2):
+        for lane in (0, 1):
+            accumulate(source, pl.ds(lane * PANEL, PANEL))
     send_across(1)
+    gate_z = {}
+    for part in (0, 1):
+        for lane in (0, 1):
+            rows = quarter(lane, part)
+            l_far[lane, part].wait_recv()
+            gzs[rows, :] = (acc[rows, :] + grad_term(1, 1, rows)).astype(BF16)
+            gate_z[lane, part] = message(gzs.at[rows, :], gz.at[rows, :], z_next)
+            gate_z[lane, part].start()
+    down_b[1].pass_on()
+    for yr in (2, 1, 3, 0):
+        down_step(yr)
+    for ring in (down_a, down_b[0]):
+        ring.far()
+        ring.near()
     for m in (0, 1):
         tr[m, 0].pass_on()
-    down_step(0)
-    gu_z = []
     for lane in (0, 1):
-        gu[1].finish(lane)
-        copy = message(pgu.at[1, 0, pl.ds(lane * PANEL, PANEL), :], gz.at[lane], z_next)
-        copy.start()
-        gu_z.append(copy)
-    down_ring.pass_on()
+        down_b[1].finish(lane)
+    down_b_z = message(pdo.at[0, pl.ds(QROWS, QROWS), :], dbz, z_next)
+    down_b_z.start()
+    down_a.pass_on()
+    down_b[0].pass_on()
+
+    @pl.loop(0, 2)
+    def _(lane):
+        rows = pl.ds(pl.multiple_of(lane * PANEL, PANEL), PANEL)
+        acc[rows, :] = grad_term(0, -1, rows) + grad_term(0, 0, rows) + grad_term(0, 1, rows) + grad_term(0, 2, rows)
 
     outs = []
     for m, out in enumerate((mixed_out, ig_out)):
@@ -474,15 +518,21 @@
         outs.append((keep, give))
 
     grads = []
+    for part in (0, 1):
+        for lane in (0, 1):
+            rows = quarter(lane, part)
+            gate_z[lane, part].wait_recv()
+            total = (acc[rows, :] + gz[rows, :].astype(F32)).astype(BF16)
+            fin[lane, :, part * QROWS:(part + 1) * QROWS] = total.T
     for lane, out in enumerate((gate_out, up_out)):
-        gu_z[lane].wait_recv()
-        gu[0].finish(lane, (gz.at[lane],))
-        gring[0, 0, lane] = pgu[0, 0, lane * PANEL:(lane + 1) * PANEL, :].T
-        copy = pltpu.make_async_copy(gring.at[0, 0, lane], out, local_sem.at[7 + lane])
+        copy = pltpu.make_async_copy(fin.at[lane], out, local_sem.at[7 + lane])
         copy.start()
         grads.append(copy)
     for lane in (0, 1):
-        down_ring.finish(lane)
+        down_a.finish(lane)
+    down_b_z.wait_recv()
+    for lane in (0, 1):
+        down_b[0].finish(lane, (dbz.at[pl.ds(lane * (QROWS // 2), QROWS // 2), :],))
     copy = pltpu.make_async_copy(wd.at[:, pl.ds(0, PANEL)], down_out, local_sem.at[9])
     copy.start()
     grads.append(copy)
@@ -523,11 +573,11 @@
             v(ROWS, PANEL), v(ROWS, PANEL), v(ROWS, PANEL),
             v(3 * PANEL, ROWS),
             pltpu.VMEM((PART, PANEL), F32), pltpu.VMEM((PART, PANEL), F32), pltpu.VMEM((PART, PANEL), F32),
-            v(ROWS, HALF), v(4, ROWS, PANEL),
-            v(2, 4, 2 * PANEL, PANEL), v(4, PANEL, PANEL),
+            v(ROWS, HALF), v(4, ROWS, PANEL), v(4, ROWS, PANEL), v(4, PANEL, PANEL),
             v(2, 2, 3, 2, BLOCK, LANE), v(2, BLOCK, HALF),
-            v(2, 3, 2, PANEL, PANEL), v(2, PANEL, PANEL),
-            v(4, PANEL, PANEL), v(3, 2, PANEL // 2, PANEL),
+            v(3, ROWS, 2 * PANEL), v(3, 2 * PANEL, ROWS),
+            pltpu.VMEM((2 * PANEL, PANEL), F32), v(2 * PANEL, PANEL), v(2 * PANEL, PANEL), v(2, PANEL, PANEL),
+            v(4, QROWS, PANEL), v(QROWS, PANEL), v(3, 3, 2, QROWS // 2, PANEL),
             v(2, 2, BLOCK // 2, HALF), v(2, 2, BLOCK // 2, HALF),
             pltpu.SemaphoreType.DMA((MESSAGES,)),
             pltpu.SemaphoreType.DMA((MESSAGES,)),

time: 144 us -> 127 us (0.88)
  Pallas kernels: 143 us -> 127 us
    pallas_call x1, Pallas kernels: 141 us -> 124 us  [on_device(): pl.pallas_call(kernel, out_shape=shapes, in_specs=[pl.BlockSpec(memory_sp...]
where the time goes in v3:
time: 127 us
  Pallas kernels  127 us (100%)
    pallas_call x1, Pallas kernels, on_device(): pl.pallas_call(kernel, out_shape=shapes, in_specs=[pl.BlockSpec(memory_sp...  124 us

profile of v3, /device:TPU:1, one launch (start us, length us, event | category | flops | bytes accessed | tf_op | source)
XLA Modules:
  0.0 127.2 jit_solution(11447988298513970585)
XLA Ops:
  0.6 124.0 %shard_map.92 = (bf16[40,4096]{1,0:T(8,128)(2,1)}, bf16[40,4096]{1,0:T(8,128)(2,1)}, bf16[512,512]{1,0:T(8,128)(2,1)}, bf16[512,512]{1,0:T(8,128)(2,1)}, bf16[512,512]{1,0:T(8,128)(2,1)}) custom-call(bf16[40,4096]{1,0:T(8,128)(2,1)} %tok_hbm.1, bf16[4096,512]{1,0:T(8,128)(2,1)} %wg_hbm.1, bf16[4096,512]{1,0:T(8,128)(2,1)} %wu_hbm.1, ...), custom_call_target="tpu_custom_call" | custom-call | flops 24199999488 | bytes 16000000 | tf_op jit(solution)/shard_map/pallas_call | solution.py:565
  124.7 2.5 %shard_map.93 = (bf16[40,4096]{1,0:T(8,128)(2,1)}, bf16[40,4096]{1,0:T(8,128)(2,1)}, bf16[512,512]{1,0:T(8,128)(2,1)}, bf16[512,512]{1,0:T(8,128)(2,1)}, bf16[512,512]{1,0:T(8,128)(2,1)}) custom-call(bf16[40,4096]{1,0:T(8,128)(2,1)} %get-tuple-element.10.refs_0_, bf16[40,4096]{1,0:T(8,128)(2,1)} %get-tuple-element.11.refs_1_, ...), custom_call_target="tpu_custom_call" | custom-call | tf_op jit(solution)/shard_map/pallas_call | solution.py:592

commit v4 on v3

--- a/solution.py
+++ b/solution.py
@@ -14,11 +14,12 @@
 PANEL = 512
 ROWS = 640
 BLOCK = 80
-PART = 320
+FIRST = 240
+MOST = 400
 MESSAGES = 160
 QROWS = PANEL // 2
 
-OWN, LEFT, RIGHT, ACROSS, FAR, ACROSS_LEFT, ACROSS_RIGHT, ACROSS_FAR = range(8)
+OWN, LEFT, ACROSS, RIGHT, FAR, ACROSS_LEFT, ACROSS_RIGHT, ACROSS_FAR = range(8)
 
 
 def mm(a, b):
@@ -50,7 +51,7 @@
     tok_hbm, wg_hbm, wu_hbm, wd_hbm, cot_hbm,
     mixed_out, ig_out, gate_out, up_out, down_out,
     wg, wu, wd, xc, hid, dg, du, lt, gf, uf, df, am, mb, sm, pdo,
-    mring, mz, ry, lty, acc, gzs, gz, fin, dz, dbz, dring, t_in, fo,
+    mring, mz, ry, lty, acc, gzs, gz, fin, dz, dbz, dring, t_in, t_next, fo,
     send_sem, recv_sem, local_sem, credit,
 ):
     dp, mp = lax.axis_index("dp"), lax.axis_index("mp")
@@ -126,23 +127,30 @@
 
     parts = [pl.ds(pl.multiple_of(c * HALF + i * LANE, LANE), LANE) for i in (0, 1)]
     to_right, to_left, to_across, relay, over = {}, {}, {}, {}, {}
+
+    def first_out(a, core):
+        copy = message(t_in.at[core, a], t_next.at[a, core], (x_right, x_left)[a])
+        copy.start()
+        return copy
+
+    def join(halves, a, slot):
+        @pl.loop(0, HALF // PANEL)
+        def _(j):
+            cols = pl.ds(pl.multiple_of(j * PANEL, PANEL), PANEL)
+            both = jnp.concatenate([halves(0)[:, cols].astype(F32), halves(1)[:, cols].astype(F32)], axis=0)
+            to = pl.ds(pl.multiple_of(c * HALF + j * PANEL, PANEL), PANEL)
+            xc[a, slot * BLOCK:(slot + 1) * BLOCK, to] = both.astype(BF16)
+
+    early = []
     for a in (0, 1):
         own_rows[a].wait()
+        early.append([first_out(a, c)])
+    for a in (0, 1):
         rows_over[a].wait_recv()
-
-        @pl.loop(0, HALF // PANEL)
-        def _(j, a=a):
-            cols = pl.ds(pl.multiple_of(j * PANEL, PANEL), PANEL)
-            both = jnp.concatenate([t_in[0, a, :, cols].astype(F32), t_in[1, a, :, cols].astype(F32)], axis=0)
-            xc[a, 0:BLOCK, pl.ds(pl.multiple_of(c * HALF + j * PANEL, PANEL), PANEL)] = both.astype(BF16)
-
+        early[a].append(first_out(a, 1 - c))
+        join(lambda core, a=a: t_in.at[core, a], a, OWN)
         to_across[a, OWN] = message(block(a, OWN), block(a, ACROSS), z_across)
-        if a == 0:
-            to_right[0, OWN] = message(block(0, OWN), block(0, LEFT), x_right)
-            to_right[0, OWN].start()
-        else:
-            to_left[1, OWN] = message(block(1, OWN), block(1, RIGHT), x_left)
-            to_left[1, OWN].start()
+        if a == 1:
             to_right[1, OWN] = [message(block(1, OWN, cols), block(1, LEFT, cols), x_right) for cols in parts]
             to_left[0, OWN] = [message(block(0, OWN, cols), block(0, RIGHT, cols), x_left) for cols in parts]
             to_right[1, OWN][0].start()
@@ -184,99 +192,102 @@
     def columns(k):
         return pl.ds(pl.multiple_of((c * 2 + k) % 4 * 1024, 1024), 1024)
 
-    def gate_up(r0, slots):
-        gf[...] = jnp.zeros_like(gf)
-        uf[...] = jnp.zeros_like(uf)
+    def gate_up(r0, count, slots):
+        span = pl.ds(r0, count)
+        gf[span, :] = jnp.zeros((count, PANEL), F32)
+        uf[span, :] = jnp.zeros((count, PANEL), F32)
 
         def step(k):
             ks = columns(k)
-            rows = xc[0, r0:r0 + PART, ks]
-            gf[...] += mm(rows, wg[ks, :])
-            uf[...] += mm(rows, wu[ks, :])
+            rows = xc[0, span, ks]
+            gf[span, :] += mm(rows, wg[ks, :])
+            uf[span, :] += mm(rows, wu[ks, :])
 
         pl.loop(0, 2)(step)
         wait_over(0, slots)
         pl.loop(2, 4)(step)
 
-        @pl.loop(0, PART // 32)
+        @pl.loop(0, count // 16)
         def _(i):
-            r = pl.ds(pl.multiple_of(i * 32, 32), 32)
-            w = pl.ds(pl.multiple_of(r0 + i * 32, 32), 32)
+            r = pl.ds(pl.multiple_of(r0 + i * 16, 16), 16)
             gate, up = gf[r, :], uf[r, :]
             s = 1.0 / (1.0 + jnp.exp(-gate))
             swish = gate * s
-            hid[w, :] = (swish * up).astype(BF16)
+            hid[r, :] = (swish * up).astype(BF16)
             gf[r, :] = up * s * (1.0 + gate * (1.0 - s))
             uf[r, :] = swish
 
-    def backward(r0, slots):
-        df[...] = jnp.zeros_like(df)
+    def backward(r0, count, slots):
+        span = pl.ds(0, count)
+        df[span, :] = jnp.zeros((count, PANEL), F32)
 
         def step(k):
             ks = columns(k)
-            df[...] += mm_nt(xc[1, r0:r0 + PART, ks], wd[:, ks])
+            df[span, :] += mm_nt(xc[1, r0:r0 + count, ks], wd[:, ks])
 
         pl.loop(0, 2)(step)
         wait_over(1, slots)
         pl.loop(2, 4)(step)
 
-        @pl.loop(0, PART // 32)
+        @pl.loop(0, count // 16)
         def _(i):
-            r = pl.ds(pl.multiple_of(i * 32, 32), 32)
-            w = pl.ds(pl.multiple_of(r0 + i * 32, 32), 32)
-            dhidden = df[r, :]
-            dg[w, :] = (dhidden * gf[r, :]).astype(BF16)
-            du[w, :] = (dhidden * uf[r, :]).astype(BF16)
-
-    def mixed_part(r0):
+            r = pl.ds(pl.multiple_of(r0 + i * 16, 16), 16)
+            dhidden = df[pl.ds(pl.multiple_of(i * 16, 16), 16), :]
+            dg[r, :] = (dhidden * gf[r, :]).astype(BF16)
+            du[r, :] = (dhidden * uf[r, :]).astype(BF16)
+
+    def mixed_sums():
         @pl.loop(0, 4)
         def _(j):
             cols = pl.ds(pl.multiple_of((1 - c) * HALF + j * PANEL, PANEL), PANEL)
-            mb[j, r0:r0 + PART, :] = mm(hid[r0:r0 + PART, :], wd[:, cols]).astype(BF16)
+            mb[j] = mm(hid[...], wd[:, cols]).astype(BF16)
 
         @pl.loop(0, 4)
         def _(j):
             cols = pl.ds(pl.multiple_of(c * HALF + j * PANEL, PANEL), PANEL)
-            total = mm(hid[r0:r0 + PART, :], wd[:, cols]).astype(BF16)
-            am[r0:r0 + PART, pl.ds(pl.multiple_of(j * PANEL, PANEL), PANEL)] = total
+            total = mm(hid[...], wd[:, cols]).astype(BF16)
+            am[:, pl.ds(pl.multiple_of(j * PANEL, PANEL), PANEL)] = total
 
     def transpose(q, src, start, stop):
         for i in range(start, stop):
             lt[q * PANEL:(q + 1) * PANEL, i * 128:(i + 1) * 128] = src[i * 128:(i + 1) * 128, :].T
 
-    to_right[0, OWN].wait_recv()
+    def first_in(a, slot):
+        for copy in early[a]:
+            copy.wait_recv()
+        join(lambda core: t_next.at[a, core], a, slot)
+
+    first_in(0, LEFT)
     relay_far(0)
     to_right[1, OWN][1].start()
-    to_left[1, OWN].wait_recv()
+    first_in(1, RIGHT)
     relay_far(1)
     to_left[0, OWN][1].start()
     over[0, LEFT] = hand_over(0, LEFT)
     over[1, RIGHT] = hand_over(1, RIGHT)
     from_across(0)
     from_across(1)
+    weights[0].wait()
+    weights[1].wait()
+    gate_up(0, FIRST, (OWN, LEFT, ACROSS))
     from_far(0)
     from_far(1)
     for a, slot, halves in ((0, RIGHT, to_left[0, OWN]), (1, LEFT, to_right[1, OWN])):
         halves[0].wait_recv()
         arrived(halves[1], a, slot)
-    near = (OWN, LEFT, RIGHT, ACROSS)
-    distant = (FAR, ACROSS_LEFT, ACROSS_RIGHT, ACROSS_FAR)
-    weights[0].wait()
-    weights[1].wait()
-    gate_up(0, near)
+    gate_up(FIRST, MOST - FIRST, (RIGHT, FAR))
     weights[2].wait()
-    backward(0, near)
+    backward(0, MOST, (OWN, LEFT, ACROSS, RIGHT, FAR))
     for q, src in enumerate((dg, du, hid)):
-        transpose(q, src, 0, 2)
+        transpose(q, src, 0, 3)
+    distant = (ACROSS_LEFT, ACROSS_RIGHT, ACROSS_FAR)
     for a in (0, 1):
         arrived(to_left[a, ACROSS], a, ACROSS_RIGHT)
         arrived(to_right[a, ACROSS], a, ACROSS_LEFT)
         arrived(to_across[a, FAR], a, ACROSS_FAR)
         if a == 0:
-            gate_up(PART, distant)
-            transpose(2, hid, 2, 5)
-            mixed_part(0)
-    backward(PART, distant)
+            gate_up(MOST, ROWS - MOST, distant)
+    backward(MOST, ROWS - MOST, distant)
     gather = list(pending)
 
     def place(z, yr):
@@ -370,18 +381,19 @@
 
     l_right = [message(half(lt, lane), half(lty.at[2], lane), y_right) for lane in (0, 1)]
     l_left = [message(half(lt, lane), half(lty.at[0], lane), y_left) for lane in (0, 1)]
-    transpose(0, dg, 2, 5)
+    transpose(0, dg, 3, 5)
     l_right[0].start()
-    transpose(1, du, 2, 5)
+    transpose(1, du, 3, 5)
     l_left[1].start()
     l_right[1].start()
     l_left[0].start()
+    transpose(2, hid, 3, 5)
     down_z = {}
     for yr in (2, 1, 3, 0):
         grad_down(1, yr)
         down_z[yr] = message(pdo.at[yr, pl.ds(0, QROWS), :], dz.at[yr], z_next)
         down_z[yr].start()
-    mixed_part(PART)
+    mixed_sums()
     mixed_over = [message(mb.at[j], sm.at[j], sibling) for j in range(4)]
     for copy in mixed_over:
         copy.start()
@@ -408,10 +420,19 @@
     ig_over = [message(xc.at[1, :, pl.ds(HALF + j * PANEL, PANEL)], sm.at[j], sibling) for j in range(4)]
     for copy in ig_over:
         copy.start()
+    tr[0, 1].pass_on()
 
     @pl.loop(0, 4)
     def _(j):
         xc[1, :, pl.ds(pl.multiple_of(j * PANEL, PANEL), PANEL)] = input_grad(c, j)
+
+    token_z = {}
+
+    def send_across(m):
+        for lane in (0, 1):
+            tr[m, 1].finish(lane)
+        token_z[m] = message(token_rows(m, ACROSS, pl.ds(0, HALF)), mz.at[m], z_across)
+        token_z[m].start()
 
     l_far = {}
     for lane, source, device in ((0, 2, y_right), (1, 0, y_left)):
@@ -420,7 +441,6 @@
             rows = quarter(lane, part)
             l_far[lane, part] = message(lty.at[source, rows, :], lty.at[1, rows, :], device)
             l_far[lane, part].start()
-    tr[0, 1].pass_on()
     for j in range(4):
         ig_over[j].wait_recv()
         add_into(xc.at[1, :, pl.ds(j * PANEL, PANEL)], sm.at[j], ROWS, 64)
@@ -428,6 +448,7 @@
     tr[1, 1].near()
     down_b[1].far()
     down_b[1].near()
+    send_across(0)
     r_over = []
     for source in (0, 2, 1):
         for slot in range(8):
@@ -443,19 +464,10 @@
     for lane in (0, 1):
         accumulate(-1, pl.ds(lane * PANEL, PANEL))
 
-    token_z = {}
-
-    def send_across(m):
-        for lane in (0, 1):
-            tr[m, 1].finish(lane)
-        token_z[m] = message(token_rows(m, ACROSS, pl.ds(0, HALF)), mz.at[m], z_across)
-        token_z[m].start()
-
     def down_step(yr):
         down_z[yr].wait_recv()
         add_into(wd.at[pl.ds(0, QROWS), pl.ds(yr * PANEL, PANEL)], dz.at[yr], QROWS, 64)
 
-    send_across(0)
     tr[1, 1].pass_on()
     for m in (0, 1):
         tr[m, 0].far()
@@ -484,17 +496,18 @@
         ring.near()
     for m in (0, 1):
         tr[m, 0].pass_on()
+
+    @pl.loop(0, 2)
+    def _(lane):
+        rows = pl.ds(pl.multiple_of(lane * PANEL, PANEL), PANEL)
+        acc[rows, :] = grad_term(0, -1, rows) + grad_term(0, 0, rows) + grad_term(0, 1, rows) + grad_term(0, 2, rows)
+
     for lane in (0, 1):
         down_b[1].finish(lane)
     down_b_z = message(pdo.at[0, pl.ds(QROWS, QROWS), :], dbz, z_next)
     down_b_z.start()
     down_a.pass_on()
     down_b[0].pass_on()
-
-    @pl.loop(0, 2)
-    def _(lane):
-        rows = pl.ds(pl.multiple_of(lane * PANEL, PANEL), PANEL)
-        acc[rows, :] = grad_term(0, -1, rows) + grad_term(0, 0, rows) + grad_term(0, 1, rows) + grad_term(0, 2, rows)
 
     outs = []
     for m, out in enumerate((mixed_out, ig_out)):
@@ -572,13 +585,13 @@
             v(2, ROWS, D),
             v(ROWS, PANEL), v(ROWS, PANEL), v(ROWS, PANEL),
             v(3 * PANEL, ROWS),
-            pltpu.VMEM((PART, PANEL), F32), pltpu.VMEM((PART, PANEL), F32), pltpu.VMEM((PART, PANEL), F32),
+            pltpu.VMEM((ROWS, PANEL), F32), pltpu.VMEM((ROWS, PANEL), F32), pltpu.VMEM((MOST, PANEL), F32),
             v(ROWS, HALF), v(4, ROWS, PANEL), v(4, ROWS, PANEL), v(4, PANEL, PANEL),
             v(2, 2, 3, 2, BLOCK, LANE), v(2, BLOCK, HALF),
             v(3, ROWS, 2 * PANEL), v(3, 2 * PANEL, ROWS),
             pltpu.VMEM((2 * PANEL, PANEL), F32), v(2 * PANEL, PANEL), v(2 * PANEL, PANEL), v(2, PANEL, PANEL),
             v(4, QROWS, PANEL), v(QROWS, PANEL), v(3, 3, 2, QROWS // 2, PANEL),
-            v(2, 2, BLOCK // 2, HALF), v(2, 2, BLOCK // 2, HALF),
+            v(2, 2, BLOCK // 2, HALF), v(2, 2, BLOCK // 2, HALF), v(2, 2, BLOCK // 2, HALF),
             pltpu.SemaphoreType.DMA((MESSAGES,)),
             pltpu.SemaphoreType.DMA((MESSAGES,)),
             pltpu.SemaphoreType.DMA((10,)),

time: 127 us -> 125 us (0.984)
  Pallas kernels: 127 us -> 124 us
    pallas_call x1, Pallas kernels: 124 us -> 121 us  [on_device(): pl.pallas_call(kernel, out_shape=shapes, in_specs=[pl.BlockSpec(memory_sp...]
where the time goes in v4:
time: 125 us
  Pallas kernels  124 us (99%)
    pallas_call x1, Pallas kernels, on_device(): pl.pallas_call(kernel, out_shape=shapes, in_specs=[pl.BlockSpec(memory_sp...  121 us

profile of v4, /device:TPU:1, one launch (start us, length us, event | category | flops | bytes accessed | tf_op | source)
XLA Modules:
  0.0 124.6 jit_solution(11040418392979936325)
XLA Ops:
  0.6 121.3 %shard_map.92 = (bf16[40,4096]{1,0:T(8,128)(2,1)}, bf16[40,4096]{1,0:T(8,128)(2,1)}, bf16[512,512]{1,0:T(8,128)(2,1)}, bf16[512,512]{1,0:T(8,128)(2,1)}, bf16[512,512]{1,0:T(8,128)(2,1)}) custom-call(bf16[40,4096]{1,0:T(8,128)(2,1)} %tok_hbm.1, bf16[4096,512]{1,0:T(8,128)(2,1)} %wg_hbm.1, bf16[4096,512]{1,0:T(8,128)(2,1)} %wu_hbm.1, ...), custom_call_target="tpu_custom_call" | custom-call | flops 24199999488 | bytes 16000000 | tf_op jit(solution)/shard_map/pallas_call | solution.py:578
  122.0 2.5 %shard_map.93 = (bf16[40,4096]{1,0:T(8,128)(2,1)}, bf16[40,4096]{1,0:T(8,128)(2,1)}, bf16[512,512]{1,0:T(8,128)(2,1)}, bf16[512,512]{1,0:T(8,128)(2,1)}, bf16[512,512]{1,0:T(8,128)(2,1)}) custom-call(bf16[40,4096]{1,0:T(8,128)(2,1)} %get-tuple-element.10.refs_0_, bf16[40,4096]{1,0:T(8,128)(2,1)} %get-tuple-element.11.refs_1_, ...), custom_call_target="tpu_custom_call" | custom-call | tf_op jit(solution)/shard_map/pallas_call | solution.py:605

commit v5 on v4

--- a/solution.py
+++ b/solution.py
@@ -194,8 +194,9 @@
 
     def gate_up(r0, count, slots):
         span = pl.ds(r0, count)
-        gf[span, :] = jnp.zeros((count, PANEL), F32)
-        uf[span, :] = jnp.zeros((count, PANEL), F32)
+        rows = xc[0, span, columns(0)]
+        gf[span, :] = mm(rows, wg[columns(0), :])
+        uf[span, :] = mm(rows, wu[columns(0), :])
 
         def step(k):
             ks = columns(k)
@@ -203,7 +204,7 @@
             gf[span, :] += mm(rows, wg[ks, :])
             uf[span, :] += mm(rows, wu[ks, :])
 
-        pl.loop(0, 2)(step)
+        step(1)
         wait_over(0, slots)
         pl.loop(2, 4)(step)
 
@@ -219,13 +220,13 @@
 
     def backward(r0, count, slots):
         span = pl.ds(0, count)
-        df[span, :] = jnp.zeros((count, PANEL), F32)
+        df[span, :] = mm_nt(xc[1, r0:r0 + count, columns(0)], wd[:, columns(0)])
 
         def step(k):
             ks = columns(k)
             df[span, :] += mm_nt(xc[1, r0:r0 + count, ks], wd[:, ks])
 
-        pl.loop(0, 2)(step)
+        step(1)
         wait_over(1, slots)
         pl.loop(2, 4)(step)
 

time: 125 us -> 124 us (level)
  no operation moved by 1% of the time
where the time goes in v5:
time: 124 us
  Pallas kernels  124 us (100%)
    pallas_call x1, Pallas kernels, on_device(): pl.pallas_call(kernel, out_shape=shapes, in_specs=[pl.BlockSpec(memory_sp...  121 us

profile of v5, /device:TPU:1, one launch (start us, length us, event | category | flops | bytes accessed | tf_op | source)
XLA Modules:
  0.0 124.3 jit_solution(6428935394893141420)
XLA Ops:
  0.6 121.1 %shard_map.92 = (bf16[40,4096]{1,0:T(8,128)(2,1)}, bf16[40,4096]{1,0:T(8,128)(2,1)}, bf16[512,512]{1,0:T(8,128)(2,1)}, bf16[512,512]{1,0:T(8,128)(2,1)}, bf16[512,512]{1,0:T(8,128)(2,1)}) custom-call(bf16[40,4096]{1,0:T(8,128)(2,1)} %tok_hbm.1, bf16[4096,512]{1,0:T(8,128)(2,1)} %wg_hbm.1, bf16[4096,512]{1,0:T(8,128)(2,1)} %wu_hbm.1, ...), custom_call_target="tpu_custom_call" | custom-call | flops 24199999488 | bytes 16000000 | tf_op jit(solution)/shard_map/pallas_call | solution.py:579
  121.7 2.5 %shard_map.93 = (bf16[40,4096]{1,0:T(8,128)(2,1)}, bf16[40,4096]{1,0:T(8,128)(2,1)}, bf16[512,512]{1,0:T(8,128)(2,1)}, bf16[512,512]{1,0:T(8,128)(2,1)}, bf16[512,512]{1,0:T(8,128)(2,1)}) custom-call(bf16[40,4096]{1,0:T(8,128)(2,1)} %get-tuple-element.10.refs_0_, bf16[40,4096]{1,0:T(8,128)(2,1)} %get-tuple-element.11.refs_1_, ...), custom_call_target="tpu_custom_call" | custom-call | tf_op jit(solution)/shard_map/pallas_call | solution.py:606

commit v6 on v5

--- a/solution.py
+++ b/solution.py
@@ -278,16 +278,19 @@
         arrived(halves[1], a, slot)
     gate_up(FIRST, MOST - FIRST, (RIGHT, FAR))
     weights[2].wait()
+
+    def arrived_across(a):
+        arrived(to_across[a, FAR], a, ACROSS_FAR)
+        arrived(to_left[a, ACROSS], a, ACROSS_RIGHT)
+        arrived(to_right[a, ACROSS], a, ACROSS_LEFT)
+
+    distant = (ACROSS_LEFT, ACROSS_RIGHT, ACROSS_FAR)
+    arrived_across(0)
     backward(0, MOST, (OWN, LEFT, ACROSS, RIGHT, FAR))
+    gate_up(MOST, ROWS - MOST, distant)
+    arrived_across(1)
     for q, src in enumerate((dg, du, hid)):
         transpose(q, src, 0, 3)
-    distant = (ACROSS_LEFT, ACROSS_RIGHT, ACROSS_FAR)
-    for a in (0, 1):
-        arrived(to_left[a, ACROSS], a, ACROSS_RIGHT)
-        arrived(to_right[a, ACROSS], a, ACROSS_LEFT)
-        arrived(to_across[a, FAR], a, ACROSS_FAR)
-        if a == 0:
-            gate_up(MOST, ROWS - MOST, distant)
     backward(MOST, ROWS - MOST, distant)
     gather = list(pending)
 

time: 124 us -> 125 us (level)
  no operation moved by 1% of the time
where the time goes in v6:
time: 125 us; the launch traced here: 124 us
  Pallas kernels  124 us (99%)
    pallas_call x1, Pallas kernels, on_device(): pl.pallas_call(kernel, out_shape=shapes, in_specs=[pl.BlockSpec(memory_sp...  121 us

profile of v6, /device:TPU:1, one launch (start us, length us, event | category | flops | bytes accessed | tf_op | source)
XLA Modules:
  0.0 124.3 jit_solution(9281966139771407952)
XLA Ops:
  0.6 121.1 %shard_map.92 = (bf16[40,4096]{1,0:T(8,128)(2,1)}, bf16[40,4096]{1,0:T(8,128)(2,1)}, bf16[512,512]{1,0:T(8,128)(2,1)}, bf16[512,512]{1,0:T(8,128)(2,1)}, bf16[512,512]{1,0:T(8,128)(2,1)}) custom-call(bf16[40,4096]{1,0:T(8,128)(2,1)} %tok_hbm.1, bf16[4096,512]{1,0:T(8,128)(2,1)} %wg_hbm.1, bf16[4096,512]{1,0:T(8,128)(2,1)} %wu_hbm.1, ...), custom_call_target="tpu_custom_call" | custom-call | flops 24199999488 | bytes 16000000 | tf_op jit(solution)/shard_map/pallas_call | solution.py:582
  121.7 2.5 %shard_map.93 = (bf16[40,4096]{1,0:T(8,128)(2,1)}, bf16[40,4096]{1,0:T(8,128)(2,1)}, bf16[512,512]{1,0:T(8,128)(2,1)}, bf16[512,512]{1,0:T(8,128)(2,1)}, bf16[512,512]{1,0:T(8,128)(2,1)}) custom-call(bf16[40,4096]{1,0:T(8,128)(2,1)} %get-tuple-element.10.refs_0_, bf16[40,4096]{1,0:T(8,128)(2,1)} %get-tuple-element.11.refs_1_, ...), custom_call_target="tpu_custom_call" | custom-call | tf_op jit(solution)/shard_map/pallas_call | solution.py:609
